TPU v7x, 512 devices: a whole 4x4x16 slice. The times are simulated.
512 devices in a mesh: req: 32 (over y, x, core), tp: 16 (over z).
Axes of the slice: x: 4, y: 4, z: 16, core: 2. Of those that a mesh axis runs over, the one named last changes fastest.
Arguments:
- queries: bfloat16 [32, 512, 16384], P('req', None, 'tp'), may hold values from -400 to 400
- kv_heads: bfloat16 [32, 16, 512, 128], P('req', None, 'tp'), may hold values from -100 to 100
- bit_widths: int32 [16], P('tp'), may hold values from 2 to 8, as said below
- destinations: int32 [32, 32, 1], P('req'), may hold values from 0 to 31; in each aligned block of 32 rows (0 to 31, 32 to 63, ..., all dimensions but the last counted through in order) at most 2 rows name the same one
- lengths: int32 [32], P('req'), may hold values from 128 to 512, as said below
Outputs:
- rotated: bfloat16 [32, 512, 16384], P('req', None, 'tp')
- page_codes: bfloat16 [32, 32, 2, 16, 16, 128], P('req', None, None, 'tp')
- page_steps: bfloat16 [32, 32, 2, 16], P('req', None, None, 'tp')
Inputs may be any that keep to these rules, and one draw needn't show every extreme that they name: `destinations`: no owner is named more than 2 times among one group's pages. `bit_widths`: each entry is 2, 4 or 8. `lengths`: some group has all 512 tokens valid.
All inputs are finite; a program needn't handle non-finite values.
Results may differ from a plain program's by a relative error of at most 0.012.
Values may be sent and summed in bfloat16 or wider, within the bound.
No kernel may reach another device: no remote copies, remote signals or barrier semaphores. Data moves between devices by JAX's collectives and lax.ppermute only.
A program may use at most 64 MiB of HBM per device.

v0:
```python
import math

import jax
import jax.numpy as jnp
from jax import lax
from jax.sharding import PartitionSpec as P

PAGE = 16


def partner(shard, axis, distance):
    return lax.ppermute(shard, axis, [(i, i ^ 1 << distance) for i in range(lax.axis_size(axis))])


def butterfly(values_now, bit_index):
    shape_now = values_now.shape
    stride = 1 << bit_index
    halves = values_now.reshape(
        shape_now[:-2] + (shape_now[-2] // (2 * stride), 2, stride, shape_now[-1])
    ).astype(jnp.float32)
    low_half = halves[..., 0, :, :]
    high_half = halves[..., 1, :, :]
    factor = math.sqrt(0.5)
    joined = jnp.stack([(low_half + high_half) * factor, (low_half - high_half) * factor], axis=-3)
    return joined.reshape(shape_now).astype(jnp.bfloat16)


def attend_local(query_block, key_rows, value_rows, length):
    kv_local, seq_len, head_dim = key_rows.shape
    group_size = query_block.shape[1] // (kv_local * head_dim)
    query_heads = query_block.reshape(seq_len, kv_local, group_size, head_dim)
    block_rows = min(256, seq_len)
    places = jnp.arange(seq_len)
    outputs = []
    for first_row in range(0, seq_len, block_rows):
        finish = first_row + block_rows
        scores = jnp.einsum(
            "qhgd,hkd->hgqk",
            query_heads[first_row:finish],
            key_rows[:, :finish],
            preferred_element_type=jnp.float32,
        ) / math.sqrt(head_dim)
        causal = (first_row + jnp.arange(block_rows))[:, None] >= jnp.arange(finish)[None, :]
        scores = jnp.where(causal, scores, -jnp.inf)
        shifted = jnp.exp(scores - jnp.max(scores, axis=-1, keepdims=True))
        weights = (shifted / jnp.sum(shifted, axis=-1, keepdims=True)).astype(jnp.bfloat16)
        outputs.append(
            jnp.einsum(
                "hgqk,hkd->qhgd",
                weights,
                value_rows[:, :finish],
                preferred_element_type=jnp.float32,
            )
        )
    attended = jnp.concatenate(outputs, axis=0)
    attended = jnp.where((places < length)[:, None, None, None], attended, 0.0).astype(jnp.bfloat16)
    return attended.reshape(seq_len, kv_local * group_size * head_dim)


def body(queries, kv_heads, bit_widths, destinations, lengths):
    length = lengths[0]
    local_kv = kv_heads[0]
    total_rows = local_kv.shape[0]
    tok_here = local_kv.shape[1]
    head_dim = local_kv.shape[2]
    tp_count = lax.axis_size("tp")
    rows_here = total_rows // tp_count
    paired = local_kv.reshape(total_rows // 2, 2, tok_here, head_dim)
    outgoing = jnp.repeat(paired, tp_count // (total_rows // 2), axis=0)
    received = lax.all_to_all(outgoing, "tp", split_axis=0, concat_axis=2, tiled=True)[0]
    seq_len = received.shape[1]
    key_rows = received[0::2]
    value_rows = received[1::2]
    own_rows = lax.dynamic_slice_in_dim(received, lax.axis_index("tp") % 2, 1, 0)
    attended = attend_local(queries[0], key_rows, value_rows, length)
    heads_here = attended.shape[1] // head_dim
    current = attended.reshape(1, seq_len, heads_here, head_dim)
    for bit_index in range(heads_here.bit_length() - 1):
        current = butterfly(current, bit_index)
    position = lax.axis_index("tp")
    factor = math.sqrt(0.5)
    for axis_bit in range(lax.axis_size("tp").bit_length() - 1):
        partner_heads = partner(current, "tp", axis_bit)
        upper_side = jnp.right_shift(position, axis_bit) % 2
        own_side = current.astype(jnp.float32)
        far_side = partner_heads.astype(jnp.float32)
        current = jnp.where(
            upper_side == 0, (own_side + far_side) * factor, (far_side - own_side) * factor
        ).astype(jnp.bfloat16)
    rotated = current.reshape(1, seq_len, heads_here * head_dim)
    pages_count = seq_len // PAGE
    owners = lax.axis_size("req")
    capacity = max(2, (3 * pages_count + 2 * owners - 1) // (2 * owners))
    places = jnp.arange(seq_len)
    live_rows = jnp.where(places[None, :, None] < length, own_rows, jnp.zeros((), jnp.bfloat16))
    page_rows = live_rows.reshape(rows_here, pages_count, PAGE, head_dim).astype(jnp.float32)
    page_rms = jnp.sqrt(jnp.mean(page_rows * page_rows, axis=(2, 3)) + 1e-06)
    page_step = (page_rms * 0.5).astype(jnp.bfloat16)
    levels = (2 ** (bit_widths - 1) - 1).astype(jnp.float32)[:, None, None, None]
    code_values = jnp.clip(
        page_rows / page_step.astype(jnp.float32)[:, :, None, None], -levels, levels
    ).astype(jnp.bfloat16)
    owner_of = destinations[0, :, 0]
    owner_ids = jnp.arange(owners, dtype=jnp.int32)
    chosen = (owner_of[:, None] == owner_ids[None, :]).astype(jnp.int32)
    earlier = jnp.cumsum(chosen, axis=0) - chosen
    slot_of = jnp.sum(earlier * chosen, axis=1)
    slot_ids = jnp.arange(capacity, dtype=jnp.int32)
    select = (
        (owner_of[None, None, :] == owner_ids[:, None, None])
        & (slot_of[None, None, :] == slot_ids[None, :, None])
    ).astype(jnp.bfloat16)
    select = select.reshape(owners * capacity, pages_count)
    flat_codes = code_values.transpose(1, 0, 2, 3).reshape(pages_count, rows_here * PAGE * head_dim)
    packed = jnp.dot(select, flat_codes, preferred_element_type=jnp.float32).astype(jnp.bfloat16)
    packed = packed.reshape(owners, capacity, rows_here, PAGE, head_dim)
    step_table = jnp.dot(select, page_step.T, preferred_element_type=jnp.float32).astype(
        jnp.bfloat16
    )
    step_table = step_table.reshape(owners, capacity, rows_here)
    got_codes, got_steps = (
        lax.all_to_all(packed, "req", split_axis=0, concat_axis=0, tiled=True),
        lax.all_to_all(step_table, "req", split_axis=0, concat_axis=0, tiled=True),
    )
    return (rotated, got_codes[None], got_steps[None])


def solution(mesh):
    in_specs = (
        P("req", None, "tp"),
        P("req", None, "tp", None),
        P("tp"),
        P("req", None, None),
        P("req"),
    )
    out_specs = (
        P("req", None, "tp"),
        P("req", None, None, "tp", None, None),
        P("req", None, None, "tp"),
    )
    return jax.shard_map(body, mesh=mesh, in_specs=in_specs, out_specs=out_specs, check_vma=False)
```

profile of v0, /device:TPU:107, one launch (start us, length us, event | category | flops | bytes accessed | tf_op | source)
XLA Modules:
  0.0 313.0 jit_solution(8405306481139989038)
XLA Ops:
  0.6 1.7 broadcast_in_dim.71
  2.3 13.7 %all-to-all-start = ((bf16[16,2,32,128]{3,2,1,0:T(8,128)(2,1)}), bf16[16,2,32,128]{3,2,1,0:T(8,128)(2,1)S(1)}, u32[]{:S(2)}, u32[]{:S(2)}) async-start(bf16[16,2,32,128]{3,2,1,0:T(8,128)(2,1)} %bitcast.2), calls=%async_computation | async-start | bytes 524288 | tf_op jit(solution)/shard_map/all_to_all | solution.py:70
  16.0 1.3 fusion.36
  18.5 14.7 %all-to-all-done = bf16[16,2,32,128]{3,2,1,0:T(8,128)(2,1)S(1)} async-done(((bf16[16,2,32,128]{3,2,1,0:T(8,128)(2,1)}), bf16[16,2,32,128]{3,2,1,0:T(8,128)(2,1)S(1)}, u32[]{:S(2)}, u32[]{:S(2)}) %all-to-all-start) | async-done | bytes 262176 | tf_op jit(solution)/shard_map/all_to_all | solution.py:70
  33.3 0.4 fusion.38
  34.0 0.6 fusion.26
  34.6 0.7 fusion.1
  35.4 0.9 fusion
  36.2 1.6 fusion.19
  39.1 1.6 multiply_convert_fusion.1
  40.7 0.7 pad_maximum_fusion.2
  41.5 1.9 collective-permute-start
  43.4 22.8 %collective-permute-done = bf16[1,512,8,128]{3,2,1,0:T(8,128)(2,1)S(1)} collective-permute-done((bf16[1,512,8,128]{3,2,1,0:T(8,128)(2,1)S(1)}, bf16[1,512,8,128]{3,2,1,0:T(8,128)(2,1)S(1)}, u32[]{:S(2)}, u32[]{:S(2)}) %collective-permute-start) | collective-permute-done | bytes 1048608 | tf_op jit(solution)/shard_map/ppermute | solution.py:12
  66.3 0.5 fusion.4
  66.8 2.9 collective-permute-start.1
  69.7 46.5 %collective-permute-done.1 = bf16[1,512,8,128]{3,2,1,0:T(8,128)(2,1)S(1)} collective-permute-done((bf16[1,512,8,128]{3,2,1,0:T(8,128)(2,1)S(1)}, bf16[1,512,8,128]{3,2,1,0:T(8,128)(2,1)S(1)}, u32[]{:S(2)}, u32[]{:S(2)}) %collective-permute-start.1) | collective-permute-done | bytes 1048608 | tf_op jit(solution)/shard_map/ppermute | solution.py:12
  116.2 0.5 fusion.8
  116.8 5.5 %collective-permute-start.2 = (bf16[1,512,8,128]{3,2,1,0:T(8,128)(2,1)S(1)}, bf16[1,512,8,128]{3,2,1,0:T(8,128)(2,1)S(1)}, u32[]{:S(2)}, u32[]{:S(2)}) collective-permute-start(bf16[1,512,8,128]{3,2,1,0:T(8,128)(2,1)S(1)} %fusion.8), channel_id=1, source_target_pairs={{0,4},{1,5},{2,6},{3,7},{4,0},{5,1},{6,2},{7,3},{8,12},{9,13},{10,... | collective-permute-start | bytes 3145736 | tf_op jit(solution)/shard_map/ppermute | solution.py:12
  123.8 107.0 %collective-permute-done.2 = bf16[1,512,8,128]{3,2,1,0:T(8,128)(2,1)S(1)} collective-permute-done((bf16[1,512,8,128]{3,2,1,0:T(8,128)(2,1)S(1)}, bf16[1,512,8,128]{3,2,1,0:T(8,128)(2,1)S(1)}, u32[]{:S(2)}, u32[]{:S(2)}) %collective-permute-start.2) | collective-permute-done | bytes 1048608 | tf_op jit(solution)/shard_map/ppermute | solution.py:12
  230.8 0.5 fusion.12
  231.4 7.5 %collective-permute-start.3 = (bf16[1,512,8,128]{3,2,1,0:T(8,128)(2,1)S(1)}, bf16[1,512,8,128]{3,2,1,0:T(8,128)(2,1)S(1)}, u32[]{:S(2)}, u32[]{:S(2)}) collective-permute-start(bf16[1,512,8,128]{3,2,1,0:T(8,128)(2,1)S(1)} %fusion.12), channel_id=1, source_target_pairs={{0,8},{1,9},{2,10},{3,11},{4,12},{5,13},{6,14},{7,15},{8,0},{9,1},... | collective-permute-start | bytes 3145736 | tf_op jit(solution)/shard_map/ppermute | solution.py:12
  239.4 0.7 reshape.400
  240.2 8.0 %all-to-all-start.2 = ((bf16[32,2,1]{1,2,0:T(2,128)(2,1)}), bf16[32,2,1]{1,2,0:T(2,128)(2,1)S(1)}, u32[]{:S(2)}, u32[]{:S(2)}) async-start(bf16[32,2,1]{1,2,0:T(2,128)(2,1)} %reshape.400), calls=%async_computation.2 | async-start | bytes 32768 | tf_op jit(solution)/shard_map/all_to_all | solution.py:123
  248.4 0.7 copy.45
  249.2 4.3 %all-to-all-done.2 = bf16[32,2,1]{1,2,0:T(2,128)(2,1)S(1)} async-done(((bf16[32,2,1]{1,2,0:T(2,128)(2,1)}), bf16[32,2,1]{1,2,0:T(2,128)(2,1)S(1)}, u32[]{:S(2)}, u32[]{:S(2)}) %all-to-all-start.2) | async-done | bytes 160 | tf_op jit(solution)/shard_map/all_to_all | solution.py:123
  253.5 5.9 %all-to-all-start.1 = ((bf16[32,2,1,16,128]{4,3,1,2,0:T(8,128)(2,1)}), bf16[32,2,1,16,128]{4,3,1,2,0:T(8,128)(2,1)S(1)}, u32[]{:S(2)}, u32[]{:S(2)}) async-start(bf16[32,2,1,16,128]{4,3,1,2,0:T(8,128)(2,1)} %bitcast.39), calls=%async_computation.1 | async-start | bytes 524288 | tf_op jit(solution)/shard_map/all_to_all | solution.py:122
  259.4 0.6 copy.35
  260.0 6.9 %all-to-all-done.1 = bf16[32,2,1,16,128]{4,3,1,2,0:T(8,128)(2,1)S(1)} async-done(((bf16[32,2,1,16,128]{4,3,1,2,0:T(8,128)(2,1)}), bf16[32,2,1,16,128]{4,3,1,2,0:T(8,128)(2,1)S(1)}, u32[]{:S(2)}, u32[]{:S(2)}) %all-to-all-start.1) | async-done | bytes 262176 | tf_op jit(solution)/shard_map/all_to_all | solution.py:122
  266.8 43.6 %collective-permute-done.3 = bf16[1,512,8,128]{3,2,1,0:T(8,128)(2,1)S(1)} collective-permute-done((bf16[1,512,8,128]{3,2,1,0:T(8,128)(2,1)S(1)}, bf16[1,512,8,128]{3,2,1,0:T(8,128)(2,1)S(1)}, u32[]{:S(2)}, u32[]{:S(2)}) %collective-permute-start.3) | collective-permute-done | bytes 1048608 | tf_op jit(solution)/shard_map/ppermute | solution.py:12
  310.4 0.5 fusion.16
  311.0 1.3 reshape.389
  312.3 0.7 copy.55
  (34 shorter events, 3.6 us)
Async XLA Ops:
  2.3 31.0 %all-to-all-start = ((bf16[16,2,32,128]{3,2,1,0:T(8,128)(2,1)}), bf16[16,2,32,128]{3,2,1,0:T(8,128)(2,1)S(1)}, u32[]{:S(2)}, u32[]{:S(2)}) async-start(bf16[16,2,32,128]{3,2,1,0:T(8,128)(2,1)} %bitcast.2), calls=%async_computation | async-start | bytes 524288 | tf_op jit(solution)/shard_map/all_to_all | solution.py:70
  41.5 24.8 %collective-permute-start = (bf16[1,512,8,128]{3,2,1,0:T(8,128)(2,1)S(1)}, bf16[1,512,8,128]{3,2,1,0:T(8,128)(2,1)S(1)}, u32[]{:S(2)}, u32[]{:S(2)}) collective-permute-start(bf16[1,512,8,128]{3,2,1,0:T(8,128)(2,1)S(1)} %bitcast.100), channel_id=1, source_target_pairs={{0,1},{1,0},{2,3},{3,2},{4,5},{5,4},{6,7},{7,6},{8,9},{9,8},{10,11... | collective-permute-start | bytes 3145736 | tf_op jit(solution)/shard_map/ppermute | solution.py:12
  66.8 56.2 %copy-start = (s32[1,32,1]{1,2,0:T(1,128)S(1)}, s32[1,32,1]{1,2,0:T(1,128)}, u32[]{:S(2)}) copy-start(s32[1,32,1]{1,2,0:T(1,128)} %param.8) | copy-start | bytes 388
  66.8 49.4 %collective-permute-start.1 = (bf16[1,512,8,128]{3,2,1,0:T(8,128)(2,1)S(1)}, bf16[1,512,8,128]{3,2,1,0:T(8,128)(2,1)S(1)}, u32[]{:S(2)}, u32[]{:S(2)}) collective-permute-start(bf16[1,512,8,128]{3,2,1,0:T(8,128)(2,1)S(1)} %fusion.4), channel_id=1, source_target_pairs={{0,2},{1,3},{2,0},{3,1},{4,6},{5,7},{6,4},{7,5},{8,10},{9,11},{10,... | collective-permute-start | bytes 3145736 | tf_op jit(solution)/shard_map/ppermute | solution.py:12
  116.8 114.1 %collective-permute-start.2 = (bf16[1,512,8,128]{3,2,1,0:T(8,128)(2,1)S(1)}, bf16[1,512,8,128]{3,2,1,0:T(8,128)(2,1)S(1)}, u32[]{:S(2)}, u32[]{:S(2)}) collective-permute-start(bf16[1,512,8,128]{3,2,1,0:T(8,128)(2,1)S(1)} %fusion.8), channel_id=1, source_target_pairs={{0,4},{1,5},{2,6},{3,7},{4,0},{5,1},{6,2},{7,3},{8,12},{9,13},{10,... | collective-permute-start | bytes 3145736 | tf_op jit(solution)/shard_map/ppermute | solution.py:12
  231.4 79.1 %collective-permute-start.3 = (bf16[1,512,8,128]{3,2,1,0:T(8,128)(2,1)S(1)}, bf16[1,512,8,128]{3,2,1,0:T(8,128)(2,1)S(1)}, u32[]{:S(2)}, u32[]{:S(2)}) collective-permute-start(bf16[1,512,8,128]{3,2,1,0:T(8,128)(2,1)S(1)} %fusion.12), channel_id=1, source_target_pairs={{0,8},{1,9},{2,10},{3,11},{4,12},{5,13},{6,14},{7,15},{8,0},{9,1},... | collective-permute-start | bytes 3145736 | tf_op jit(solution)/shard_map/ppermute | solution.py:12
  240.2 13.3 %all-to-all-start.2 = ((bf16[32,2,1]{1,2,0:T(2,128)(2,1)}), bf16[32,2,1]{1,2,0:T(2,128)(2,1)S(1)}, u32[]{:S(2)}, u32[]{:S(2)}) async-start(bf16[32,2,1]{1,2,0:T(2,128)(2,1)} %reshape.400), calls=%async_computation.2 | async-start | bytes 32768 | tf_op jit(solution)/shard_map/all_to_all | solution.py:123
  253.5 13.4 %all-to-all-start.1 = ((bf16[32,2,1,16,128]{4,3,1,2,0:T(8,128)(2,1)}), bf16[32,2,1,16,128]{4,3,1,2,0:T(8,128)(2,1)S(1)}, u32[]{:S(2)}, u32[]{:S(2)}) async-start(bf16[32,2,1,16,128]{4,3,1,2,0:T(8,128)(2,1)} %bitcast.39), calls=%async_computation.1 | async-start | bytes 524288 | tf_op jit(solution)/shard_map/all_to_all | solution.py:122
where the time goes:
time: 313 us
  waiting for transfers between devices  246 us (79%)
  starting transfers between devices  45.5 us (15%)
  local copies, waits for them, and re-layouts  7.91 us (3%)
  other arithmetic  7.8 us (2%)
  matrix products  3.7 us (1%)
    ppermute x4, waiting for transfers between devices, partner(): lax.ppermute(shard, axis, [(i, i ^ 1 << distance) for i in range(lax.axis...  220 us
    ppermute x4, starting transfers between devices, partner(): lax.ppermute(shard, axis, [(i, i ^ 1 << distance) for i in range(lax.axis...  17.8 us
    all_to_all x1, waiting for transfers between devices, body(): lax.all_to_all(outgoing, 'tp', split_axis=0, concat_axis=2, tiled=True)[0]  14.7 us
    all_to_all x1, starting transfers between devices, body(): lax.all_to_all(outgoing, 'tp', split_axis=0, concat_axis=2, tiled=True)[0]  13.7 us
    all_to_all x1, starting transfers between devices, body(): lax.all_to_all(step_table, 'req', split_axis=0, concat_axis=0, tiled=True)  8.05 us
    all_to_all x1, waiting for transfers between devices, body(): lax.all_to_all(packed, 'req', split_axis=0, concat_axis=0, tiled=True)  6.88 us
  transfers between devices with their start and end apart: 7, of which 7 were waited for; matrix products, arithmetic and copies ran while one was open for 2% of the time, Pallas kernels for 0%

commit v1 on v0

v1 whole, which is shorter than its diff:
```python
import math

import jax
import jax.numpy as jnp
from jax import lax
from jax.sharding import PartitionSpec as P

PAGE = 16


def sign_matrix(count):
    row = lax.broadcasted_iota(jnp.int32, (count, count), 0)
    col = lax.broadcasted_iota(jnp.int32, (count, count), 1)
    both = row & col
    parity = jnp.zeros_like(both)
    for bit in range(count.bit_length() - 1):
        parity = parity ^ (jnp.right_shift(both, bit) & 1)
    return (1 - 2 * parity).astype(jnp.bfloat16)


def attend_local(query_block, key_rows, value_rows, length, heads):
    seq_len, head_dim = key_rows.shape
    query_heads = query_block.reshape(seq_len, heads, head_dim)
    block_rows = min(256, seq_len)
    places = jnp.arange(seq_len)
    outputs = []
    for first_row in range(0, seq_len, block_rows):
        finish = first_row + block_rows
        scores = jnp.einsum(
            "qgd,kd->gqk",
            query_heads[first_row:finish],
            key_rows[:finish],
            preferred_element_type=jnp.float32,
        ) / math.sqrt(head_dim)
        causal = (first_row + jnp.arange(block_rows))[:, None] >= jnp.arange(finish)[None, :]
        scores = jnp.where(causal, scores, -jnp.inf)
        shifted = jnp.exp(scores - jnp.max(scores, axis=-1, keepdims=True))
        weights = (shifted / jnp.sum(shifted, axis=-1, keepdims=True)).astype(jnp.bfloat16)
        outputs.append(
            jnp.einsum(
                "gqk,kd->gqd",
                weights,
                value_rows[:finish],
                preferred_element_type=jnp.float32,
            )
        )
    attended = jnp.concatenate(outputs, axis=1)
    return jnp.where((places < length)[None, :, None], attended, 0.0).astype(jnp.bfloat16)


def body(queries, kv_heads, bit_widths, destinations, lengths):
    length = lengths[0]
    local_kv = kv_heads[0]
    total_rows, tok_here, head_dim = local_kv.shape
    tp_count = lax.axis_size("tp")
    rows_here = total_rows // tp_count
    paired = local_kv.reshape(total_rows // 2, 2, tok_here, head_dim)
    outgoing = jnp.repeat(paired, tp_count // (total_rows // 2), axis=0)
    received = lax.all_to_all(outgoing, "tp", split_axis=0, concat_axis=2, tiled=True)[0]
    seq_len = received.shape[1]
    own_rows = lax.dynamic_slice_in_dim(received, lax.axis_index("tp") % 2, 1, 0)
    heads_here = queries.shape[2] // head_dim
    attended = attend_local(queries[0], received[0], received[1], length, heads_here)

    share = seq_len // tp_count
    blocks = attended.reshape(heads_here, tp_count, share, head_dim).transpose(1, 0, 2, 3)
    blocks = lax.all_to_all(blocks, "tp", split_axis=0, concat_axis=0, tiled=True)
    all_heads = tp_count * heads_here
    mixed = jnp.dot(
        sign_matrix(all_heads),
        blocks.reshape(all_heads, share * head_dim),
        preferred_element_type=jnp.float32,
    ) * (1.0 / math.sqrt(all_heads))
    mixed = mixed.astype(jnp.bfloat16).reshape(tp_count, heads_here, share, head_dim)
    back = lax.all_to_all(mixed, "tp", split_axis=0, concat_axis=0, tiled=True)
    rotated = back.transpose(0, 2, 1, 3).reshape(1, seq_len, heads_here * head_dim)

    pages_count = seq_len // PAGE
    owners = lax.axis_size("req")
    capacity = max(2, (3 * pages_count + 2 * owners - 1) // (2 * owners))
    places = jnp.arange(seq_len)
    live_rows = jnp.where(places[None, :, None] < length, own_rows, jnp.zeros((), jnp.bfloat16))
    page_rows = live_rows.reshape(rows_here, pages_count, PAGE, head_dim).astype(jnp.float32)
    page_rms = jnp.sqrt(jnp.mean(page_rows * page_rows, axis=(2, 3)) + 1e-06)
    page_step = (page_rms * 0.5).astype(jnp.bfloat16)
    levels = (2 ** (bit_widths - 1) - 1).astype(jnp.float32)[:, None, None, None]
    code_values = jnp.clip(
        page_rows / page_step.astype(jnp.float32)[:, :, None, None], -levels, levels
    ).astype(jnp.bfloat16)
    owner_of = destinations[0, :, 0]
    owner_ids = jnp.arange(owners, dtype=jnp.int32)
    chosen = (owner_of[:, None] == owner_ids[None, :]).astype(jnp.int32)
    earlier = jnp.cumsum(chosen, axis=0) - chosen
    slot_of = jnp.sum(earlier * chosen, axis=1)
    slot_ids = jnp.arange(capacity, dtype=jnp.int32)
    select = (
        (owner_of[None, None, :] == owner_ids[:, None, None])
        & (slot_of[None, None, :] == slot_ids[None, :, None])
    ).astype(jnp.bfloat16)
    select = select.reshape(owners * capacity, pages_count)
    width = rows_here * PAGE * head_dim
    flat_codes = code_values.transpose(1, 0, 2, 3).reshape(pages_count, width)
    steps_wide = jnp.broadcast_to(page_step.T[:, :, None], (pages_count, rows_here, head_dim))
    flat = jnp.concatenate([flat_codes, steps_wide.reshape(pages_count, -1)], axis=1)
    packed = jnp.dot(select, flat, preferred_element_type=jnp.float32).astype(jnp.bfloat16)
    packed = packed.reshape(owners, capacity, -1)
    got = lax.all_to_all(packed, "req", split_axis=0, concat_axis=0, tiled=True)
    got_codes = got[:, :, :width].reshape(owners, capacity, rows_here, PAGE, head_dim)
    got_steps = got[:, :, width:].reshape(owners, capacity, rows_here, head_dim)[..., 0]
    return (rotated, got_codes[None], got_steps[None])


def solution(mesh):
    in_specs = (
        P("req", None, "tp"),
        P("req", None, "tp", None),
        P("tp"),
        P("req", None, None),
        P("req"),
    )
    out_specs = (
        P("req", None, "tp"),
        P("req", None, None, "tp", None, None),
        P("req", None, None, "tp"),
    )
    return jax.shard_map(body, mesh=mesh, in_specs=in_specs, out_specs=out_specs, check_vma=False)
```

time: 313 us -> 180 us (0.58)
  the two profiles are of different devices: /device:TPU:107 before, /device:TPU:32 now
where the time goes in v1:
time: 180 us; the launch traced here: 179 us
  waiting for transfers between devices  117 us (65%)
  starting transfers between devices  37.5 us (21%)
  matrix products  12.3 us (7%)
  local copies, waits for them, and re-layouts  7.36 us (4%)
  other arithmetic  2.42 us (1%)
  between operations  2.16 us (1%)
    all_to_all x1, waiting for transfers between devices, body(): back = lax.all_to_all(mixed, 'tp', split_axis=0, concat_axis=0, tiled=True)  48.3 us
    all_to_all x1, waiting for transfers between devices, body(): lax.all_to_all(blocks, 'tp', split_axis=0, concat_axis=0, tiled=True)  46.1 us
    all_to_all x1, waiting for transfers between devices, body(): lax.all_to_all(outgoing, 'tp', split_axis=0, concat_axis=2, tiled=True)[0]  15.4 us
    all_to_all x1, starting transfers between devices, body(): lax.all_to_all(outgoing, 'tp', split_axis=0, concat_axis=2, tiled=True)[0]  15.2 us
    all_to_all x1, starting transfers between devices, body(): back = lax.all_to_all(mixed, 'tp', split_axis=0, concat_axis=0, tiled=True)  8.68 us
    all_to_all x1, waiting for transfers between devices, body(): got = lax.all_to_all(packed, 'req', split_axis=0, concat_axis=0, tiled=True)  7.51 us
    all_to_all x1, starting transfers between devices, body(): got = lax.all_to_all(packed, 'req', split_axis=0, concat_axis=0, tiled=True)  7.32 us
    all_to_all x1, starting transfers between devices, body(): lax.all_to_all(blocks, 'tp', split_axis=0, concat_axis=0, tiled=True)  6.26 us
  transfers between devices with their start and end apart: 4, of which 4 were waited for; matrix products, arithmetic and copies ran while one was open for 4% of the time, Pallas kernels for 0%

profile of v1, /device:TPU:32, one launch (start us, length us, event | category | flops | bytes accessed | tf_op | source)
XLA Modules:
  0.0 179.1 jit_solution(4230905819926292136)
XLA Ops:
  0.6 1.7 broadcast_in_dim.68
  2.3 15.2 %all-to-all-start = ((bf16[16,2,32,128]{3,2,1,0:T(8,128)(2,1)}), bf16[16,2,32,128]{3,2,1,0:T(8,128)(2,1)S(1)}, u32[]{:S(2)}, u32[]{:S(2)}) async-start(bf16[16,2,32,128]{3,2,1,0:T(8,128)(2,1)} %bitcast.2), calls=%async_computation | async-start | bytes 524288 | tf_op jit(solution)/shard_map/all_to_all | solution.py:59
  17.5 1.3 fusion.46
  18.8 0.2 copy.47
  19.0 0.2 copy.46
  19.9 0.1 iota_compare_fusion
  20.0 15.4 %all-to-all-done = bf16[16,2,32,128]{3,2,1,0:T(8,128)(2,1)S(1)} async-done(((bf16[16,2,32,128]{3,2,1,0:T(8,128)(2,1)}), bf16[16,2,32,128]{3,2,1,0:T(8,128)(2,1)S(1)}, u32[]{:S(2)}, u32[]{:S(2)}) %all-to-all-start) | async-done | bytes 262176 | tf_op jit(solution)/shard_map/all_to_all | solution.py:59
  35.5 3.3 %fusion.50 = (f32[8,256]{1,0:T(8,128)S(1)}, f32[8,256,512]{1,2,0:T(8,128)}) fusion(pred[256,512]{0,1:T(8,128)(4,1)S(1)} %iota_compare_fusion, bf16[512,128,1]{1,0,2:T(8,128)(2,1)S(1)} %bitcast.84, bf16[256,8,128]{0,2,1:T(8,128)(2,1)S(1)} %bitcast.80), kind=kOutput, calls=%fused_computation.75 | convolution fusion | flops 272630272 | bytes 4988928 | tf_op jit(solution)/shard_map/sub | solution.py:37
  38.8 3.0 %fusion.7 = bf16[8,256,128]{2,1,0:T(8,128)(2,1)S(1)} fusion(bf16[512,128,1]{1,0,2:T(8,128)(2,1)S(1)} %bitcast.83, f32[8,256,512]{1,2,0:T(8,128)} %get-tuple-element.22, f32[8,256]{1,0:T(8,128)S(1)} %get-tuple-element.21), kind=kOutput, calls=%fused_computation.17 | convolution fusion | flops 270532608 | bytes 4857856 | tf_op jit(solution)/shard_map/gqk,kd->gqd/dot_general | solution.py:40
  41.8 2.1 %fusion.51 = (f32[8,256]{1,0:T(8,128)S(1)}, f32[8,256,256]{1,2,0:T(8,128)}) fusion(pred[256,256]{0,1:T(8,128)(4,1)S(1)} %iota_compare_fusion.1, bf16[256,128,1]{1,0,2:T(8,128)(2,1)S(1)} %bitcast.87, bf16[256,8,128]{0,2,1:T(8,128)(2,1)S(1)} %bitcast.79), kind=kOutput, calls=%fused_computation.76 | convolution fusion | flops 136315136 | bytes 2760704 | tf_op jit(solution)/shard_map/sub | solution.py:37
  43.9 2.1 %fusion.16 = bf16[8,256,128]{2,1,0:T(8,128)(2,1)S(1)} fusion(bf16[256,128,1]{1,0,2:T(8,128)(2,1)S(1)} %bitcast.86, f32[8,256,256]{1,2,0:T(8,128)} %get-tuple-element.24, f32[8,256]{1,0:T(8,128)S(1)} %get-tuple-element.23), kind=kOutput, calls=%fused_computation.26 | convolution fusion | flops 135266304 | bytes 2695168 | tf_op jit(solution)/shard_map/gqk,kd->gqd/dot_general | solution.py:40
  46.1 1.3 fusion.11
  47.3 6.3 %all-to-all-start.1 = ((bf16[16,8,32,128]{3,2,1,0:T(8,128)(2,1)}), bf16[16,8,32,128]{3,2,1,0:T(8,128)(2,1)S(1)}, u32[]{:S(2)}, u32[]{:S(2)}) async-start(bf16[16,8,32,128]{3,2,1,0:T(8,128)(2,1)} %fusion.11), calls=%async_computation.1 | async-start | bytes 2097152 | tf_op jit(solution)/shard_map/all_to_all | solution.py:67
  54.2 0.1 iota_compare_fusion.3
  54.4 0.2 select_reduce_fusion
  54.7 0.2 multiply_reduce_fusion
  54.9 0.1 reduce_sum.47
  55.0 0.1 select_convert_fusion
  55.2 0.1 reduce_sum.48
  55.3 0.1 minimum_convert_fusion
  55.5 0.2 convolution_convert_fusion
  55.8 0.8 reshape.168
  56.6 46.1 %all-to-all-done.1 = bf16[16,8,32,128]{3,2,1,0:T(8,128)(2,1)S(1)} async-done(((bf16[16,8,32,128]{3,2,1,0:T(8,128)(2,1)}), bf16[16,8,32,128]{3,2,1,0:T(8,128)(2,1)S(1)}, u32[]{:S(2)}, u32[]{:S(2)}) %all-to-all-start.1) | async-done | bytes 1048608 | tf_op jit(solution)/shard_map/all_to_all | solution.py:67
  102.7 7.3 %all-to-all-start.3 = ((bf16[32,2,2176]{2,1,0:T(2,128)(2,1)}), bf16[32,2,2176]{2,1,0:T(2,128)(2,1)S(1)}, u32[]{:S(2)}, u32[]{:S(2)}) async-start(bf16[32,2,2176]{2,1,0:T(2,128)(2,1)} %reshape.168), calls=%async_computation.3 | async-start | bytes 557056 | tf_op jit(solution)/shard_map/all_to_all | solution.py:107
  110.0 1.6 fusion.10
  111.6 7.5 %all-to-all-done.3 = bf16[32,2,2176]{2,1,0:T(2,128)(2,1)S(1)} async-done(((bf16[32,2,2176]{2,1,0:T(2,128)(2,1)}), bf16[32,2,2176]{2,1,0:T(2,128)(2,1)S(1)}, u32[]{:S(2)}, u32[]{:S(2)}) %all-to-all-start.3) | async-done | bytes 278560 | tf_op jit(solution)/shard_map/all_to_all | solution.py:107
  119.1 8.7 %all-to-all-start.2 = ((bf16[16,8,32,128]{3,1,2,0:T(8,128)(2,1)}), bf16[16,8,32,128]{3,1,2,0:T(8,128)(2,1)S(1)}, u32[]{:S(2)}, u32[]{:S(2)}) async-start(bf16[16,8,32,128]{3,1,2,0:T(8,128)(2,1)} %fusion.10), calls=%async_computation.2 | async-start | bytes 2097152 | tf_op jit(solution)/shard_map/all_to_all | solution.py:75
  127.8 0.2 slice.60
  128.0 0.9 broadcast_in_dim_reshape.3
  128.8 0.6 copy.40
  129.5 48.3 %all-to-all-done.2 = bf16[16,8,32,128]{3,1,2,0:T(8,128)(2,1)S(1)} async-done(((bf16[16,8,32,128]{3,1,2,0:T(8,128)(2,1)}), bf16[16,8,32,128]{3,1,2,0:T(8,128)(2,1)S(1)}, u32[]{:S(2)}, u32[]{:S(2)}) %all-to-all-start.2) | async-done | bytes 1048608 | tf_op jit(solution)/shard_map/all_to_all | solution.py:75
  177.8 1.3 reshape.166
  (18 shorter events, 0.4 us)
Async XLA Ops:
  2.3 33.1 %all-to-all-start = ((bf16[16,2,32,128]{3,2,1,0:T(8,128)(2,1)}), bf16[16,2,32,128]{3,2,1,0:T(8,128)(2,1)S(1)}, u32[]{:S(2)}, u32[]{:S(2)}) async-start(bf16[16,2,32,128]{3,2,1,0:T(8,128)(2,1)} %bitcast.2), calls=%async_computation | async-start | bytes 524288 | tf_op jit(solution)/shard_map/all_to_all | solution.py:59
  46.0 8.2 %copy-start = (s32[1,32,1]{1,2,0:T(1,128)S(1)}, s32[1,32,1]{1,2,0:T(1,128)}, u32[]{:S(2)}) copy-start(s32[1,32,1]{1,2,0:T(1,128)} %param.8) | copy-start | bytes 388
  47.3 55.4 %all-to-all-start.1 = ((bf16[16,8,32,128]{3,2,1,0:T(8,128)(2,1)}), bf16[16,8,32,128]{3,2,1,0:T(8,128)(2,1)S(1)}, u32[]{:S(2)}, u32[]{:S(2)}) async-start(bf16[16,8,32,128]{3,2,1,0:T(8,128)(2,1)} %fusion.11), calls=%async_computation.1 | async-start | bytes 2097152 | tf_op jit(solution)/shard_map/all_to_all | solution.py:67
  102.7 16.4 %all-to-all-start.3 = ((bf16[32,2,2176]{2,1,0:T(2,128)(2,1)}), bf16[32,2,2176]{2,1,0:T(2,128)(2,1)S(1)}, u32[]{:S(2)}, u32[]{:S(2)}) async-start(bf16[32,2,2176]{2,1,0:T(2,128)(2,1)} %reshape.168), calls=%async_computation.3 | async-start | bytes 557056 | tf_op jit(solution)/shard_map/all_to_all | solution.py:107
  119.1 58.7 %all-to-all-start.2 = ((bf16[16,8,32,128]{3,1,2,0:T(8,128)(2,1)}), bf16[16,8,32,128]{3,1,2,0:T(8,128)(2,1)S(1)}, u32[]{:S(2)}, u32[]{:S(2)}) async-start(bf16[16,8,32,128]{3,1,2,0:T(8,128)(2,1)} %fusion.10), calls=%async_computation.2 | async-start | bytes 2097152 | tf_op jit(solution)/shard_map/all_to_all | solution.py:75

commit v2 on v1

v2 whole, which is shorter than its diff:
```python
import functools
import math

import jax
import jax.numpy as jnp
from jax import lax
from jax.experimental import pallas as pl
from jax.experimental.pallas import tpu as pltpu
from jax.sharding import PartitionSpec as P

PAGE = 16
BLOCK = 128


def attend_kernel(length_ref, q_ref, kv_ref, out_ref, k_ref, v_ref, *, blocks, heads):
    head_dim = k_ref.shape[1]
    seq_len = k_ref.shape[0]
    step = pl.program_id(0)

    @pl.when(step == 0)
    def _():
        k_ref[...] = kv_ref[:, 0].reshape(seq_len, head_dim)
        v_ref[:, :head_dim] = kv_ref[:, 1].reshape(seq_len, head_dim)
        v_ref[:, head_dim:] = jnp.ones((seq_len, head_dim), jnp.bfloat16)

    rate = math.log2(math.e) / math.sqrt(head_dim)
    rows = lax.broadcasted_iota(jnp.int32, (BLOCK, BLOCK), 0)
    cols = lax.broadcasted_iota(jnp.int32, (BLOCK, BLOCK), 1)
    causal = rows >= cols
    live = step * BLOCK + lax.broadcasted_iota(jnp.int32, (BLOCK, head_dim), 0) < length_ref[0]

    def attend(index):
        finish = (index + 1) * BLOCK
        for head in range(heads):
            columns = slice(head * head_dim, (head + 1) * head_dim)
            scores = lax.dot_general(
                q_ref[:, columns],
                k_ref[:finish],
                (((1,), (1,)), ((), ())),
                preferred_element_type=jnp.float32,
            )
            last = jnp.where(causal, scores[:, index * BLOCK :], -jnp.inf)
            if index:
                scores = jnp.concatenate([scores[:, : index * BLOCK], last], axis=1)
            else:
                scores = last
            top = jnp.max(scores, axis=1, keepdims=True)
            weights = jnp.exp2((scores - top) * rate).astype(jnp.bfloat16)
            both = jnp.dot(weights, v_ref[:finish], preferred_element_type=jnp.float32)
            attended = both[:, :head_dim] / both[:, head_dim:]
            out_ref[:, columns] = jnp.where(live, attended, 0.0).astype(jnp.bfloat16)

    for index in range(blocks):
        pl.when(step == index)(functools.partial(attend, index))


def attend_local(queries, received, length, head_dim):
    seq_len, width = queries.shape
    heads = width // head_dim
    blocks = seq_len // BLOCK
    return pl.pallas_call(
        functools.partial(attend_kernel, blocks=blocks, heads=heads),
        grid=(blocks,),
        in_specs=[
            pl.BlockSpec(memory_space=pltpu.SMEM),
            pl.BlockSpec((BLOCK, width), lambda i: (i, 0)),
            pl.BlockSpec(received.shape, lambda i: (0, 0, 0, 0)),
        ],
        out_specs=pl.BlockSpec((BLOCK, width), lambda i: (i, 0)),
        out_shape=jax.ShapeDtypeStruct((seq_len, width), jnp.bfloat16),
        scratch_shapes=[
            pltpu.VMEM((seq_len, head_dim), jnp.bfloat16),
            pltpu.VMEM((seq_len, 2 * head_dim), jnp.bfloat16),
        ],
        compiler_params=pltpu.CompilerParams(vmem_limit_bytes=32 * 1024 * 1024),
        cost_estimate=pl.CostEstimate(
            flops=4 * seq_len * seq_len * width,
            bytes_accessed=4 * seq_len * width,
            transcendentals=seq_len * seq_len * heads,
        ),
        name="attend",
    )(length, queries, received)


def butterflies(values):
    values = list(values)
    stride = 1
    while stride < len(values):
        for low in range(len(values)):
            if not low & stride:
                a, b = values[low], values[low + stride]
                values[low], values[low + stride] = a + b, a - b
        stride *= 2
    return values


def hadamard_kernel(in_ref, out_ref, mid_ref, *, heads):
    devices, tokens, width = in_ref.shape
    head_dim = width // heads
    factor = 1.0 / math.sqrt(devices * heads)
    columns = [slice(h * head_dim, (h + 1) * head_dim) for h in range(heads)]
    for first in range(0, tokens, PAGE):
        rows = slice(first, first + PAGE)
        for device in range(devices):
            tiles = butterflies([in_ref[device, rows, c].astype(jnp.float32) for c in columns])
            for c, tile in zip(columns, tiles):
                mid_ref[device, :, c] = tile
        for c in columns:
            tiles = butterflies([mid_ref[device, :, c] for device in range(devices)])
            for device, tile in enumerate(tiles):
                out_ref[device, rows, c] = (tile * factor).astype(jnp.bfloat16)


def hadamard(blocks, heads):
    devices, tokens, width = blocks.shape
    spec = pl.BlockSpec((devices, PAGE, width), lambda i: (0, i, 0))
    return pl.pallas_call(
        functools.partial(hadamard_kernel, heads=heads),
        grid=(tokens // PAGE,),
        in_specs=[spec],
        out_specs=spec,
        out_shape=jax.ShapeDtypeStruct(blocks.shape, jnp.bfloat16),
        scratch_shapes=[pltpu.VMEM((devices, PAGE, width), jnp.float32)],
        compiler_params=pltpu.CompilerParams(vmem_limit_bytes=32 * 1024 * 1024),
        cost_estimate=pl.CostEstimate(
            flops=7 * blocks.size, bytes_accessed=4 * blocks.size, transcendentals=0
        ),
        name="hadamard",
    )(blocks)


def pick_kernel(which_ref, filled_ref, every_ref, out_ref, sems, *, capacity):
    count = out_ref.shape[0]

    def copy(item):
        first = pl.multiple_of(which_ref[item] * PAGE, PAGE)
        return pltpu.make_async_copy(
            every_ref.at[item // capacity, pl.ds(first, PAGE)], out_ref.at[item], sems.at[item]
        )

    for item in range(count):
        copy(item).start()
    for item in range(count):
        copy(item).wait()
        page = out_ref[item]
        out_ref[item] = jnp.where(filled_ref[item] > 0, page, jnp.zeros_like(page))


def pick_pages(every, which, filled, capacity):
    count = which.shape[0]
    head_dim = every.shape[2]
    smem = pl.BlockSpec(memory_space=pltpu.SMEM)
    return pl.pallas_call(
        functools.partial(pick_kernel, capacity=capacity),
        in_specs=[smem, smem, pl.BlockSpec(memory_space=pl.ANY)],
        out_specs=pl.BlockSpec(memory_space=pltpu.VMEM),
        out_shape=jax.ShapeDtypeStruct((count, PAGE, head_dim), jnp.bfloat16),
        scratch_shapes=[pltpu.SemaphoreType.DMA((count,))],
        cost_estimate=pl.CostEstimate(
            flops=0, bytes_accessed=4 * count * PAGE * head_dim, transcendentals=0
        ),
        name="pick_pages",
    )(which, filled, every)


def page_parts(own_rows, bit_widths, owner_of, length):
    seq_len, head_dim = own_rows.shape
    pages = seq_len // PAGE
    places = jnp.arange(seq_len)
    live_rows = jnp.where(places[:, None] < length, own_rows, jnp.zeros((), jnp.bfloat16))
    page_rows = live_rows.reshape(pages, PAGE, head_dim).astype(jnp.float32)
    page_rms = jnp.sqrt(jnp.mean(page_rows * page_rows, axis=(1, 2)) + 1e-06)
    page_step = (page_rms * 0.5).astype(jnp.bfloat16)
    level = (2 ** (bit_widths[0] - 1) - 1).astype(jnp.float32)
    codes = jnp.clip(page_rows / page_step.astype(jnp.float32)[:, None, None], -level, level)
    page_ids = jnp.arange(pages)
    same = (owner_of[:, None] == owner_of[None, :]) & (page_ids[None, :] < page_ids[:, None])
    slot_of = jnp.sum(same.astype(jnp.int32), axis=1)
    return codes.astype(jnp.bfloat16), page_step, slot_of


def body(queries, kv_heads, bit_widths, destinations, lengths):
    length = lengths[0]
    local_kv = kv_heads[0]
    total_rows, tok_here, head_dim = local_kv.shape
    tp_count = lax.axis_size("tp")
    owners = lax.axis_size("req")
    paired = local_kv.reshape(total_rows // 2, 2, tok_here, head_dim)
    outgoing = jnp.repeat(paired, tp_count // (total_rows // 2), axis=0)
    received = lax.all_to_all(outgoing, "tp", split_axis=0, concat_axis=0, tiled=True)
    seq_len = tp_count * tok_here
    heads_here = queries.shape[2] // head_dim

    attended = attend_local(queries[0], received, lengths, head_dim)
    blocks = attended.reshape(tp_count, seq_len // tp_count, heads_here * head_dim)
    blocks = lax.all_to_all(blocks, "tp", split_axis=0, concat_axis=0, tiled=True)
    mixed = hadamard(blocks, heads_here)
    back = lax.all_to_all(mixed, "tp", split_axis=0, concat_axis=0, tiled=True)
    rotated = back.reshape(1, seq_len, heads_here * head_dim)

    pages = seq_len // PAGE
    capacity = max(2, (3 * pages + 2 * owners - 1) // (2 * owners))
    own_rows = lax.dynamic_index_in_dim(received, lax.axis_index("tp") % 2, 1, keepdims=False)
    own_rows = own_rows.reshape(seq_len, head_dim)
    codes, steps, slots = page_parts(own_rows, bit_widths, destinations[0, :, 0], length)
    target = destinations[0, :, 0] * capacity + slots
    extra = jnp.broadcast_to(
        jnp.stack([steps, target.astype(jnp.bfloat16)])[:, :, None], (2, pages, head_dim)
    )
    sent = jnp.concatenate([codes.reshape(seq_len, head_dim), extra.reshape(2 * pages, head_dim)])
    every = lax.all_gather(sent, "req", axis=0, tiled=False)
    every_steps = every[:, seq_len : seq_len + pages, 0]
    every_target = every[:, seq_len + pages :, 0].astype(jnp.int32)
    mine = lax.axis_index("req") * capacity + jnp.arange(capacity)
    select = (every_target[:, None, :] == mine[None, :, None]).astype(jnp.int32)
    which = jnp.sum(select * jnp.arange(pages), axis=2).reshape(owners * capacity)
    filled = jnp.sum(select, axis=2)
    got_codes = pick_pages(every, which, filled.reshape(owners * capacity), capacity)
    got_steps = jnp.sum(
        select.astype(jnp.float32) * every_steps.astype(jnp.float32)[:, None, :], axis=2
    ).astype(jnp.bfloat16)
    return (
        rotated,
        got_codes.reshape(1, owners, capacity, 1, PAGE, head_dim),
        got_steps.reshape(1, owners, capacity, 1),
    )


def solution(mesh):
    in_specs = (
        P("req", None, "tp"),
        P("req", None, "tp", None),
        P("tp"),
        P("req", None, None),
        P("req"),
    )
    out_specs = (
        P("req", None, "tp"),
        P("req", None, None, "tp", None, None),
        P("req", None, None, "tp"),
    )
    return jax.shard_map(body, mesh=mesh, in_specs=in_specs, out_specs=out_specs, check_vma=False)
```

time: 180 us -> 182 us (1.011)
  the two profiles are of different devices: /device:TPU:32 before, /device:TPU:30 now
where the time goes in v2:
time: 182 us; the launch traced here: 181 us
  waiting for transfers between devices  65.1 us (36%)
  blocking collectives  57.1 us (31%)
  starting transfers between devices  21.5 us (12%)
  between operations  15.4 us (8%)
  Pallas kernels  9.77 us (5%)
  other arithmetic  6.67 us (4%)
  local copies, waits for them, and re-layouts  5.8 us (3%)
    all_to_all x1, blocking collectives, body(): lax.all_to_all(blocks, 'tp', split_axis=0, concat_axis=0, tiled=True)  57.1 us
    all_to_all x1, waiting for transfers between devices, body(): back = lax.all_to_all(mixed, 'tp', split_axis=0, concat_axis=0, tiled=True)  49.9 us
    all_to_all x1, starting transfers between devices, body(): lax.all_to_all(outgoing, 'tp', split_axis=0, concat_axis=0, tiled=True)  15.2 us
    all_to_all x1, waiting for transfers between devices, body(): lax.all_to_all(outgoing, 'tp', split_axis=0, concat_axis=0, tiled=True)  15.1 us
    all_to_all x1, starting transfers between devices, body(): back = lax.all_to_all(mixed, 'tp', split_axis=0, concat_axis=0, tiled=True)  6.29 us
    pallas_call x1, Pallas kernels, attend_local(): pl.pallas_call(functools.partial(attend_kernel, blocks=blocks, heads=head...  4.81 us
  transfers between devices with their start and end apart: 3, of which 2 were waited for; matrix products, arithmetic and copies ran while one was open for 1% of the time, Pallas kernels for 4%

profile of v2, /device:TPU:30, one launch (start us, length us, event | category | flops | bytes accessed | tf_op | source)
XLA Modules:
  0.0 181.4 jit_solution(288230579883297425)
XLA Ops:
  7.2 1.7 broadcast_in_dim.35
  8.8 15.2 %all-to-all-start = ((bf16[16,2,32,128]{3,2,1,0:T(8,128)(2,1)}), bf16[16,2,32,128]{3,2,1,0:T(8,128)(2,1)S(1)}, u32[]{:S(2)}, u32[]{:S(2)}) async-start(bf16[16,2,32,128]{3,2,1,0:T(8,128)(2,1)} %bitcast.2), calls=%async_computation | async-start | bytes 524288 | tf_op jit(solution)/shard_map/all_to_all | solution.py:190
  25.4 0.1 iota.66
  25.5 0.1 iota.67
  25.6 0.1 iota.57
  25.7 0.9 convert_reduce_fusion.3
  26.6 0.7 fusion.4
  27.3 15.1 %all-to-all-done.kv_ref = bf16[16,2,32,128]{3,2,1,0:T(8,128)(2,1)S(1)} async-done(((bf16[16,2,32,128]{3,2,1,0:T(8,128)(2,1)}), bf16[16,2,32,128]{3,2,1,0:T(8,128)(2,1)S(1)}, u32[]{:S(2)}, u32[]{:S(2)}) %all-to-all-start) | async-done | bytes 262176 | tf_op jit(solution)/shard_map/all_to_all | solution.py:190
  42.4 0.3 multiply_reduce_fusion
  42.6 0.1 reduce_sum.55
  42.7 0.1 reduce_sum.56
  42.9 0.1 div.21
  42.9 0.1 div.22
  43.0 0.1 reshape.199
  43.1 0.2 minimum_convert_fusion
  43.3 0.8 pad_maximum_fusion
  44.2 1.2 copy-done
  45.4 4.8 %attend.1 = bf16[512,1024]{1,0:T(8,128)(2,1)S(1)} custom-call(s32[1]{0:T(128)} %copy.15.length_ref, bf16[512,1024]{1,0:T(8,128)(2,1)S(1)} %bitcast.35, bf16[16,2,32,128]{3,2,1,0:T(8,128)(2,1)S(1)} %all-to-all-done.kv_ref), custom_call_target="tpu_custom_call" | custom-call | flops 1073741824 | bytes 2097152 | tf_op jit(solution)/shard_map/attend/pallas_call | solution.py:61
  50.2 57.1 %all_to_all.15.in_ref = bf16[16,32,1024]{2,1,0:T(8,128)(2,1)S(1)} all-to-all(bf16[16,32,1024]{2,1,0:T(8,128)(2,1)S(1)} %bitcast.34), channel_id=1, replica_groups=mesh['req'=32,'tp'=16] {'tp'}, dimensions={0} | all-to-all | bytes 2097152 | tf_op jit(solution)/shard_map/all_to_all | solution.py:196
  107.3 1.8 hadamard.1
  109.1 6.3 %all-to-all-start.2 = ((bf16[16,32,1024]{2,1,0:T(8,128)(2,1)}), bf16[16,32,1024]{2,1,0:T(8,128)(2,1)S(1)}, u32[]{:S(2)}, u32[]{:S(2)}) async-start(bf16[16,32,1024]{2,1,0:T(8,128)(2,1)} %hadamard.1), calls=%async_computation.2 | async-start | bytes 2097152 | tf_op jit(solution)/shard_map/all_to_all | solution.py:198
  115.4 49.9 %all-to-all-done.2 = bf16[16,32,1024]{2,1,0:T(8,128)(2,1)S(1)} async-done(((bf16[16,32,1024]{2,1,0:T(8,128)(2,1)}), bf16[16,32,1024]{2,1,0:T(8,128)(2,1)S(1)}, u32[]{:S(2)}, u32[]{:S(2)}) %all-to-all-start.2) | async-done | bytes 1048608 | tf_op jit(solution)/shard_map/all_to_all | solution.py:198
  165.3 1.2 convert_reduce_fusion
  166.5 1.6 convert_reduce_fusion.1
  168.1 0.2 convert_reduce_fusion.2
  168.3 0.7 fusion.2
  169.0 0.1 copy.10
  169.1 0.6 reshape.173.which_ref
  169.7 0.1 copy.11
  169.8 0.6 reshape.174.filled_ref
  170.4 3.2 %pick_pages.1 = bf16[64,16,128]{2,1,0:T(8,128)(2,1)} custom-call(s32[64]{0:T(128)} %reshape.173.which_ref, s32[64]{0:T(128)} %reshape.174.filled_ref, bf16[32,576,128]{2,1,0:T(8,128)(2,1)} %bitcast.38), custom_call_target="tpu_custom_call" | custom-call | bytes 524288 | tf_op jit(solution)/shard_map/pick_pages/pallas_call | solution.py:153
  173.5 1.0 copy.16
  (12 shorter events, 0.1 us)
Async XLA Ops:
  8.8 33.6 %all-to-all-start = ((bf16[16,2,32,128]{3,2,1,0:T(8,128)(2,1)}), bf16[16,2,32,128]{3,2,1,0:T(8,128)(2,1)S(1)}, u32[]{:S(2)}, u32[]{:S(2)}) async-start(bf16[16,2,32,128]{3,2,1,0:T(8,128)(2,1)} %bitcast.2), calls=%async_computation | async-start | bytes 524288 | tf_op jit(solution)/shard_map/all_to_all | solution.py:190
  24.0 141.3 %all-gather.3.cloned.1.call-start = ((), (), s32[]{:S(2)}) async-start(), calls=%async_computation.3 | async-start | bytes 4866048 | tf_op jit(solution)/shard_map/all_gather | solution.py:211
  44.2 1.2 copy-start
  109.1 56.2 %all-to-all-start.2 = ((bf16[16,32,1024]{2,1,0:T(8,128)(2,1)}), bf16[16,32,1024]{2,1,0:T(8,128)(2,1)S(1)}, u32[]{:S(2)}, u32[]{:S(2)}) async-start(bf16[16,32,1024]{2,1,0:T(8,128)(2,1)} %hadamard.1), calls=%async_computation.2 | async-start | bytes 2097152 | tf_op jit(solution)/shard_map/all_to_all | solution.py:198
Sparse Core Ops, SparseCore 0:
  44.3 54.7 all-gather.2

commit v3 on v2

--- a/solution.py
+++ b/solution.py
@@ -129,58 +129,79 @@
     )(blocks)
 
 
-def pick_kernel(which_ref, filled_ref, every_ref, out_ref, sems, *, capacity):
-    count = out_ref.shape[0]
-
-    def copy(item):
-        first = pl.multiple_of(which_ref[item] * PAGE, PAGE)
-        return pltpu.make_async_copy(
-            every_ref.at[item // capacity, pl.ds(first, PAGE)], out_ref.at[item], sems.at[item]
-        )
-
-    for item in range(count):
-        copy(item).start()
-    for item in range(count):
-        copy(item).wait()
-        page = out_ref[item]
-        out_ref[item] = jnp.where(filled_ref[item] > 0, page, jnp.zeros_like(page))
-
-
-def pick_pages(every, which, filled, capacity):
-    count = which.shape[0]
-    head_dim = every.shape[2]
+def page_kernel(
+    length_ref, level_ref, side_ref, owner_ref, kv_ref, out_ref, count_ref, *, owners, capacity
+):
+    sources, _, tokens, head_dim = kv_ref.shape
+    out_ref[...] = jnp.zeros_like(out_ref)
+    for owner in range(owners):
+        count_ref[owner] = 0
+    level = level_ref[0].astype(jnp.float32)
+    side = side_ref[0]
+    rows = lax.broadcasted_iota(jnp.int32, (PAGE, head_dim), 0)
+    tail = lax.broadcasted_iota(jnp.int32, (8, head_dim), 0)
+    per_source = tokens // PAGE
+
+    def one_page(page, _):
+        source = page // per_source
+        first = (page % per_source) * PAGE
+        values = kv_ref[source, side, pl.ds(pl.multiple_of(first, PAGE), PAGE), :]
+        live = page * PAGE + rows < length_ref[0]
+        values = jnp.where(live, values.astype(jnp.float32), 0.0)
+        total = jnp.sum(values * values, axis=(0, 1), keepdims=True)
+        rms = jnp.sqrt(total / (PAGE * head_dim) + 1e-06)
+        step = (rms * 0.5).astype(jnp.bfloat16).astype(jnp.float32)
+        codes = jnp.clip(values / step, -level, level).astype(jnp.bfloat16)
+        owner = owner_ref[page]
+        slot = jnp.minimum(count_ref[owner], capacity - 1)
+        count_ref[owner] = slot + 1
+        out_ref[owner, pl.ds(pl.multiple_of(slot * PAGE, PAGE), PAGE), :] = codes
+        before = out_ref[owner, capacity * PAGE :, :].astype(jnp.float32)
+        steps = jnp.where(tail == slot, jnp.broadcast_to(step, tail.shape), before)
+        out_ref[owner, capacity * PAGE :, :] = steps.astype(jnp.bfloat16)
+        return 0
+
+    lax.fori_loop(0, sources * per_source, one_page, 0)
+
+
+def page_table(received, length, level, owner_of, owners, capacity):
+    head_dim = received.shape[3]
     smem = pl.BlockSpec(memory_space=pltpu.SMEM)
+    vmem = pl.BlockSpec(memory_space=pltpu.VMEM)
+    side = (lax.axis_index("tp") % 2).astype(jnp.int32).reshape(1)
+    shape = (owners, capacity * PAGE + 8, head_dim)
     return pl.pallas_call(
-        functools.partial(pick_kernel, capacity=capacity),
-        in_specs=[smem, smem, pl.BlockSpec(memory_space=pl.ANY)],
-        out_specs=pl.BlockSpec(memory_space=pltpu.VMEM),
-        out_shape=jax.ShapeDtypeStruct((count, PAGE, head_dim), jnp.bfloat16),
-        scratch_shapes=[pltpu.SemaphoreType.DMA((count,))],
+        functools.partial(page_kernel, owners=owners, capacity=capacity),
+        in_specs=[smem, smem, smem, smem, vmem],
+        out_specs=vmem,
+        out_shape=jax.ShapeDtypeStruct(shape, jnp.bfloat16),
+        scratch_shapes=[pltpu.SMEM((owners,), jnp.int32)],
+        compiler_params=pltpu.CompilerParams(vmem_limit_bytes=32 * 1024 * 1024),
         cost_estimate=pl.CostEstimate(
-            flops=0, bytes_accessed=4 * count * PAGE * head_dim, transcendentals=0
+            flops=10 * received.size, bytes_accessed=2 * received.size, transcendentals=0
         ),
-        name="pick_pages",
-    )(which, filled, every)
-
-
-def page_parts(own_rows, bit_widths, owner_of, length):
-    seq_len, head_dim = own_rows.shape
-    pages = seq_len // PAGE
-    places = jnp.arange(seq_len)
-    live_rows = jnp.where(places[:, None] < length, own_rows, jnp.zeros((), jnp.bfloat16))
-    page_rows = live_rows.reshape(pages, PAGE, head_dim).astype(jnp.float32)
-    page_rms = jnp.sqrt(jnp.mean(page_rows * page_rows, axis=(1, 2)) + 1e-06)
-    page_step = (page_rms * 0.5).astype(jnp.bfloat16)
-    level = (2 ** (bit_widths[0] - 1) - 1).astype(jnp.float32)
-    codes = jnp.clip(page_rows / page_step.astype(jnp.float32)[:, None, None], -level, level)
-    page_ids = jnp.arange(pages)
-    same = (owner_of[:, None] == owner_of[None, :]) & (page_ids[None, :] < page_ids[:, None])
-    slot_of = jnp.sum(same.astype(jnp.int32), axis=1)
-    return codes.astype(jnp.bfloat16), page_step, slot_of
+        name="pages",
+    )(length, level, side, owner_of, received)
+
+
+def to_owners(table, axis):
+    count = lax.axis_size(axis)
+    position = lax.axis_index(axis)
+    inner = table.shape[1:]
+    for bit in range(count.bit_length() - 1):
+        stride = 1 << bit
+        upper = jnp.right_shift(position, bit) % 2
+        halves = table.reshape((count // (2 * stride), 2, stride) + inner)
+        keep = lax.dynamic_index_in_dim(halves, upper, 1, keepdims=False)
+        send = lax.dynamic_index_in_dim(halves, 1 - upper, 1, keepdims=False)
+        got = lax.ppermute(send, axis, [(i, i ^ stride) for i in range(count)])
+        low = jnp.where(upper == 0, keep, got)
+        high = jnp.where(upper == 0, got, keep)
+        table = jnp.stack([low, high], axis=1).reshape((count,) + inner)
+    return table
 
 
 def body(queries, kv_heads, bit_widths, destinations, lengths):
-    length = lengths[0]
     local_kv = kv_heads[0]
     total_rows, tok_here, head_dim = local_kv.shape
     tp_count = lax.axis_size("tp")
@@ -200,30 +221,12 @@
 
     pages = seq_len // PAGE
     capacity = max(2, (3 * pages + 2 * owners - 1) // (2 * owners))
-    own_rows = lax.dynamic_index_in_dim(received, lax.axis_index("tp") % 2, 1, keepdims=False)
-    own_rows = own_rows.reshape(seq_len, head_dim)
-    codes, steps, slots = page_parts(own_rows, bit_widths, destinations[0, :, 0], length)
-    target = destinations[0, :, 0] * capacity + slots
-    extra = jnp.broadcast_to(
-        jnp.stack([steps, target.astype(jnp.bfloat16)])[:, :, None], (2, pages, head_dim)
-    )
-    sent = jnp.concatenate([codes.reshape(seq_len, head_dim), extra.reshape(2 * pages, head_dim)])
-    every = lax.all_gather(sent, "req", axis=0, tiled=False)
-    every_steps = every[:, seq_len : seq_len + pages, 0]
-    every_target = every[:, seq_len + pages :, 0].astype(jnp.int32)
-    mine = lax.axis_index("req") * capacity + jnp.arange(capacity)
-    select = (every_target[:, None, :] == mine[None, :, None]).astype(jnp.int32)
-    which = jnp.sum(select * jnp.arange(pages), axis=2).reshape(owners * capacity)
-    filled = jnp.sum(select, axis=2)
-    got_codes = pick_pages(every, which, filled.reshape(owners * capacity), capacity)
-    got_steps = jnp.sum(
-        select.astype(jnp.float32) * every_steps.astype(jnp.float32)[:, None, :], axis=2
-    ).astype(jnp.bfloat16)
-    return (
-        rotated,
-        got_codes.reshape(1, owners, capacity, 1, PAGE, head_dim),
-        got_steps.reshape(1, owners, capacity, 1),
-    )
+    level = 2 ** (bit_widths - 1) - 1
+    table = page_table(received, lengths, level, destinations[0, :, 0], owners, capacity)
+    table = to_owners(table, "req")
+    got_codes = table[:, : capacity * PAGE].reshape(1, owners, capacity, 1, PAGE, head_dim)
+    got_steps = table[:, capacity * PAGE : capacity * (PAGE + 1), 0]
+    return rotated, got_codes, got_steps.reshape(1, owners, capacity, 1)
 
 
 def solution(mesh):

time: 182 us -> 159 us (0.87)
  the two profiles are of different devices: /device:TPU:30 before, /device:TPU:2 now
where the time goes in v3:
time: 159 us; the launch traced here: 158 us
  blocking collectives  57.1 us (36%)
  waiting for transfers between devices  41.9 us (26%)
  starting transfers between devices  38.5 us (24%)
  Pallas kernels  12 us (8%)
  local copies, waits for them, and re-layouts  6.01 us (4%)
  between operations  2.28 us (1%)
    all_to_all x1, blocking collectives, body(): lax.all_to_all(blocks, 'tp', split_axis=0, concat_axis=0, tiled=True)  57.1 us
    ppermute x5, waiting for transfers between devices, to_owners(): got = lax.ppermute(send, axis, [(i, i ^ stride) for i in range(count)])  19.1 us
    all_to_all x1, waiting for transfers between devices, body(): lax.all_to_all(outgoing, 'tp', split_axis=0, concat_axis=0, tiled=True)  17.7 us
    ppermute x5, starting transfers between devices, to_owners(): got = lax.ppermute(send, axis, [(i, i ^ stride) for i in range(count)])  17 us
    all_to_all x1, starting transfers between devices, body(): lax.all_to_all(outgoing, 'tp', split_axis=0, concat_axis=0, tiled=True)  15.2 us
    all_to_all x1, starting transfers between devices, body(): back = lax.all_to_all(mixed, 'tp', split_axis=0, concat_axis=0, tiled=True)  6.29 us
    pallas_call x1, Pallas kernels, page_table(): pl.pallas_call(functools.partial(page_kernel, owners=owners, capacity=cap...  5.36 us
    all_to_all x1, waiting for transfers between devices, body(): back = lax.all_to_all(mixed, 'tp', split_axis=0, concat_axis=0, tiled=True)  5.09 us
  transfers between devices with their start and end apart: 7, of which 7 were waited for; matrix products, arithmetic and copies ran while one was open for 1% of the time, Pallas kernels for 3%

profile of v3, /device:TPU:2, one launch (start us, length us, event | category | flops | bytes accessed | tf_op | source)
XLA Modules:
  0.0 158.0 jit_solution(10809913159715747039)
XLA Ops:
  0.6 1.7 %broadcast_in_dim.7 = bf16[8,2,2,32,128]{4,3,2,1,0:T(8,128)(2,1)} broadcast(bf16[8,2,32,128]{3,2,1,0:T(8,128)(2,1)} %bitcast.96), dimensions={0,2,3,4} | broadcast | bytes 393216 | tf_op jit(solution)/shard_map/broadcast_in_dim | solution.py:210
  2.3 15.2 %all-to-all-start = ((bf16[16,2,32,128]{3,2,1,0:T(8,128)(2,1)}), bf16[16,2,32,128]{3,2,1,0:T(8,128)(2,1)S(1)}, u32[]{:S(2)}, u32[]{:S(2)}) async-start(bf16[16,2,32,128]{3,2,1,0:T(8,128)(2,1)} %bitcast.2), calls=%async_computation | async-start | bytes 524288 | tf_op jit(solution)/shard_map/all_to_all | solution.py:211
  18.1 17.7 %all-to-all-done.kv_ref = bf16[16,2,32,128]{3,2,1,0:T(8,128)(2,1)S(1)} async-done(((bf16[16,2,32,128]{3,2,1,0:T(8,128)(2,1)}), bf16[16,2,32,128]{3,2,1,0:T(8,128)(2,1)S(1)}, u32[]{:S(2)}, u32[]{:S(2)}) %all-to-all-start) | async-done | bytes 262176 | tf_op jit(solution)/shard_map/all_to_all | solution.py:211
  35.9 0.0 copy-start.1
  35.9 1.2 copy-done.1
  37.1 4.8 %attend.1 = bf16[512,1024]{1,0:T(8,128)(2,1)S(1)} custom-call(s32[1]{0:T(128)S(6)} %copy.38.length_ref, bf16[512,1024]{1,0:T(8,128)(2,1)S(1)} %bitcast.82, bf16[16,2,32,128]{3,2,1,0:T(8,128)(2,1)S(1)} %all-to-all-done.kv_ref), custom_call_target="tpu_custom_call" | custom-call | flops 1073741824 | bytes 2097152 | tf_op jit(solution)/shard_map/attend/pallas_call | solution.py:61
  41.9 57.1 %all_to_all.15.in_ref = bf16[16,32,1024]{2,1,0:T(8,128)(2,1)S(1)} all-to-all(bf16[16,32,1024]{2,1,0:T(8,128)(2,1)S(1)} %bitcast.80), channel_id=1, replica_groups=mesh['req'=32,'tp'=16] {'tp'}, dimensions={0} | all-to-all | bytes 2097152 | tf_op jit(solution)/shard_map/all_to_all | solution.py:217
  99.0 1.8 %hadamard.1 = bf16[16,32,1024]{2,1,0:T(8,128)(2,1)} custom-call(bf16[16,32,1024]{2,1,0:T(8,128)(2,1)S(1)} %all_to_all.15.in_ref), custom_call_target="tpu_custom_call" | custom-call | flops 3670016 | bytes 2097152 | tf_op jit(solution)/shard_map/hadamard/pallas_call | solution.py:117
  100.8 6.3 %all-to-all-start.2 = ((bf16[16,32,1024]{2,1,0:T(8,128)(2,1)}), bf16[16,32,1024]{2,1,0:T(8,128)(2,1)S(1)}, u32[]{:S(2)}, u32[]{:S(2)}) async-start(bf16[16,32,1024]{2,1,0:T(8,128)(2,1)} %hadamard.1), calls=%async_computation.2 | async-start | bytes 2097152 | tf_op jit(solution)/shard_map/all_to_all | solution.py:219
  107.8 0.0 copy-start
  107.8 0.6 copy-done
  108.4 5.4 %pages.1 = bf16[32,40,128]{2,1,0:T(8,128)(2,1)S(1)} custom-call(s32[1]{0:T(128)S(6)} %copy.38.length_ref, s32[1]{0:T(128)S(6)} %sub.22.level_ref, s32[1]{0:T(128)} %bitcast.5.side_ref, s32[32]{0:T(128)S(1)} %bitcast.81, bf16[16,2,32,128]{3,2,1,0:T(8,128)(2,1)S(1)} %all-to-all-done.kv_ref), custom_call_target="tpu_custom_call" | custom-call | flops 1310720 | bytes 262144 | tf_op jit(solution)/shard_map/pages/pallas_call | solution.py:173
  113.8 1.9 %collective-permute-start = (bf16[16,1,40,128]{3,2,0,1:T(8,128)(2,1)S(1)}, bf16[16,1,40,128]{3,2,0,1:T(8,128)(2,1)S(1)}, u32[]{:S(2)}, u32[]{:S(2)}) collective-permute-start(bf16[16,1,40,128]{3,2,0,1:T(8,128)(2,1)S(1)} %dynamic-slice_bitcast_fusion.3), channel_id=1, source_target_pairs={{0,16},{16,0},{32,48},{48,32},{64,80},{80,64},{96,112},{112,96},{1... | collective-permute-start | bytes 491528 | tf_op jit(solution)/shard_map/ppermute | solution.py:197
  115.8 1.3 collective-permute-done
  117.2 2.4 %collective-permute-start.1 = (bf16[8,2,40,128]{3,2,1,0:T(8,128)(2,1)S(1)}, bf16[8,2,40,128]{3,2,1,0:T(8,128)(2,1)S(1)}, u32[]{:S(2)}, u32[]{:S(2)}) collective-permute-start(bf16[8,2,40,128]{3,2,1,0:T(8,128)(2,1)S(1)} %bitcast.95), channel_id=1, source_target_pairs={{0,32},{16,48},{32,0},{48,16},{64,96},{80,112},{96,64},{112,80},{1... | collective-permute-start | bytes 491528 | tf_op jit(solution)/shard_map/ppermute | solution.py:197
  119.7 5.7 %collective-permute-done.1 = bf16[8,2,40,128]{3,2,1,0:T(8,128)(2,1)S(1)} collective-permute-done((bf16[8,2,40,128]{3,2,1,0:T(8,128)(2,1)S(1)}, bf16[8,2,40,128]{3,2,1,0:T(8,128)(2,1)S(1)}, u32[]{:S(2)}, u32[]{:S(2)}) %collective-permute-start.1) | collective-permute-done | bytes 163872 | tf_op jit(solution)/shard_map/ppermute | solution.py:197
  125.5 4.0 %collective-permute-start.2 = (bf16[4,4,40,128]{3,2,1,0:T(8,128)(2,1)S(1)}, bf16[4,4,40,128]{3,2,1,0:T(8,128)(2,1)S(1)}, u32[]{:S(2)}, u32[]{:S(2)}) collective-permute-start(bf16[4,4,40,128]{3,2,1,0:T(8,128)(2,1)S(1)} %dynamic-slice_bitcast_fusion.2), channel_id=1, source_target_pairs={{0,64},{16,80},{32,96},{48,112},{64,0},{80,16},{96,32},{112,48},{1... | collective-permute-start | bytes 491528 | tf_op jit(solution)/shard_map/ppermute | solution.py:197
  129.6 4.8 %collective-permute-done.2 = bf16[4,4,40,128]{3,2,1,0:T(8,128)(2,1)S(1)} collective-permute-done((bf16[4,4,40,128]{3,2,1,0:T(8,128)(2,1)S(1)}, bf16[4,4,40,128]{3,2,1,0:T(8,128)(2,1)S(1)}, u32[]{:S(2)}, u32[]{:S(2)}) %collective-permute-start.2) | collective-permute-done | bytes 163872 | tf_op jit(solution)/shard_map/ppermute | solution.py:197
  134.4 3.5 %collective-permute-start.3 = (bf16[2,8,40,128]{3,2,1,0:T(8,128)(2,1)S(1)}, bf16[2,8,40,128]{3,2,1,0:T(8,128)(2,1)S(1)}, u32[]{:S(2)}, u32[]{:S(2)}) collective-permute-start(bf16[2,8,40,128]{3,2,1,0:T(8,128)(2,1)S(1)} %dynamic-slice_bitcast_fusion.1), channel_id=1, source_target_pairs={{0,128},{16,144},{32,160},{48,176},{64,192},{80,208},{96,224},{112... | collective-permute-start | bytes 491528 | tf_op jit(solution)/shard_map/ppermute | solution.py:197
  138.0 3.7 %collective-permute-done.3 = bf16[2,8,40,128]{3,2,1,0:T(8,128)(2,1)S(1)} collective-permute-done((bf16[2,8,40,128]{3,2,1,0:T(8,128)(2,1)S(1)}, bf16[2,8,40,128]{3,2,1,0:T(8,128)(2,1)S(1)}, u32[]{:S(2)}, u32[]{:S(2)}) %collective-permute-start.3) | collective-permute-done | bytes 163872 | tf_op jit(solution)/shard_map/ppermute | solution.py:197
  141.8 5.1 %collective-permute-start.4 = (bf16[1,16,40,128]{3,2,1,0:T(8,128)(2,1)S(1)}, bf16[1,16,40,128]{3,2,1,0:T(8,128)(2,1)S(1)}, u32[]{:S(2)}, u32[]{:S(2)}) collective-permute-start(bf16[1,16,40,128]{3,2,1,0:T(8,128)(2,1)S(1)} %dynamic-slice_bitcast_fusion), channel_id=1, source_target_pairs={{0,256},{16,272},{32,288},{48,304},{64,320},{80,336},{96,352},{112... | collective-permute-start | bytes 491528 | tf_op jit(solution)/shard_map/ppermute | solution.py:197
  146.9 3.6 %collective-permute-done.4 = bf16[1,16,40,128]{3,2,1,0:T(8,128)(2,1)S(1)} collective-permute-done((bf16[1,16,40,128]{3,2,1,0:T(8,128)(2,1)S(1)}, bf16[1,16,40,128]{3,2,1,0:T(8,128)(2,1)S(1)}, u32[]{:S(2)}, u32[]{:S(2)}) %collective-permute-start.4) | collective-permute-done | bytes 163872 | tf_op jit(solution)/shard_map/ppermute | solution.py:197
  150.6 0.7 slice.8
  151.3 0.6 copy.30
  151.9 5.1 %all-to-all-done.2 = bf16[16,32,1024]{2,1,0:T(8,128)(2,1)S(1)} async-done(((bf16[16,32,1024]{2,1,0:T(8,128)(2,1)}), bf16[16,32,1024]{2,1,0:T(8,128)(2,1)S(1)}, u32[]{:S(2)}, u32[]{:S(2)}) %all-to-all-start.2) | async-done | bytes 1048608 | tf_op jit(solution)/shard_map/all_to_all | solution.py:219
  157.0 1.0 copy.39
  (18 shorter events, 0.5 us)
Async XLA Ops:
  2.3 33.6 %all-to-all-start = ((bf16[16,2,32,128]{3,2,1,0:T(8,128)(2,1)}), bf16[16,2,32,128]{3,2,1,0:T(8,128)(2,1)S(1)}, u32[]{:S(2)}, u32[]{:S(2)}) async-start(bf16[16,2,32,128]{3,2,1,0:T(8,128)(2,1)} %bitcast.2), calls=%async_computation | async-start | bytes 524288 | tf_op jit(solution)/shard_map/all_to_all | solution.py:211
  35.9 1.2 copy-start.1
  100.8 56.2 %all-to-all-start.2 = ((bf16[16,32,1024]{2,1,0:T(8,128)(2,1)}), bf16[16,32,1024]{2,1,0:T(8,128)(2,1)S(1)}, u32[]{:S(2)}, u32[]{:S(2)}) async-start(bf16[16,32,1024]{2,1,0:T(8,128)(2,1)} %hadamard.1), calls=%async_computation.2 | async-start | bytes 2097152 | tf_op jit(solution)/shard_map/all_to_all | solution.py:219
  107.8 0.7 copy-start
  113.8 3.3 %collective-permute-start = (bf16[16,1,40,128]{3,2,0,1:T(8,128)(2,1)S(1)}, bf16[16,1,40,128]{3,2,0,1:T(8,128)(2,1)S(1)}, u32[]{:S(2)}, u32[]{:S(2)}) collective-permute-start(bf16[16,1,40,128]{3,2,0,1:T(8,128)(2,1)S(1)} %dynamic-slice_bitcast_fusion.3), channel_id=1, source_target_pairs={{0,16},{16,0},{32,48},{48,32},{64,80},{80,64},{96,112},{112,96},{1... | collective-permute-start | bytes 491528 | tf_op jit(solution)/shard_map/ppermute | solution.py:197
  117.2 8.1 %collective-permute-start.1 = (bf16[8,2,40,128]{3,2,1,0:T(8,128)(2,1)S(1)}, bf16[8,2,40,128]{3,2,1,0:T(8,128)(2,1)S(1)}, u32[]{:S(2)}, u32[]{:S(2)}) collective-permute-start(bf16[8,2,40,128]{3,2,1,0:T(8,128)(2,1)S(1)} %bitcast.95), channel_id=1, source_target_pairs={{0,32},{16,48},{32,0},{48,16},{64,96},{80,112},{96,64},{112,80},{1... | collective-permute-start | bytes 491528 | tf_op jit(solution)/shard_map/ppermute | solution.py:197
  125.5 8.8 %collective-permute-start.2 = (bf16[4,4,40,128]{3,2,1,0:T(8,128)(2,1)S(1)}, bf16[4,4,40,128]{3,2,1,0:T(8,128)(2,1)S(1)}, u32[]{:S(2)}, u32[]{:S(2)}) collective-permute-start(bf16[4,4,40,128]{3,2,1,0:T(8,128)(2,1)S(1)} %dynamic-slice_bitcast_fusion.2), channel_id=1, source_target_pairs={{0,64},{16,80},{32,96},{48,112},{64,0},{80,16},{96,32},{112,48},{1... | collective-permute-start | bytes 491528 | tf_op jit(solution)/shard_map/ppermute | solution.py:197
  134.4 7.2 %collective-permute-start.3 = (bf16[2,8,40,128]{3,2,1,0:T(8,128)(2,1)S(1)}, bf16[2,8,40,128]{3,2,1,0:T(8,128)(2,1)S(1)}, u32[]{:S(2)}, u32[]{:S(2)}) collective-permute-start(bf16[2,8,40,128]{3,2,1,0:T(8,128)(2,1)S(1)} %dynamic-slice_bitcast_fusion.1), channel_id=1, source_target_pairs={{0,128},{16,144},{32,160},{48,176},{64,192},{80,208},{96,224},{112... | collective-permute-start | bytes 491528 | tf_op jit(solution)/shard_map/ppermute | solution.py:197
  141.8 8.7 %collective-permute-start.4 = (bf16[1,16,40,128]{3,2,1,0:T(8,128)(2,1)S(1)}, bf16[1,16,40,128]{3,2,1,0:T(8,128)(2,1)S(1)}, u32[]{:S(2)}, u32[]{:S(2)}) collective-permute-start(bf16[1,16,40,128]{3,2,1,0:T(8,128)(2,1)S(1)} %dynamic-slice_bitcast_fusion), channel_id=1, source_target_pairs={{0,256},{16,272},{32,288},{48,304},{64,320},{80,336},{96,352},{112... | collective-permute-start | bytes 491528 | tf_op jit(solution)/shard_map/ppermute | solution.py:197

commit v4 on v3

--- a/solution.py
+++ b/solution.py
@@ -9,10 +9,12 @@
 from jax.sharding import PartitionSpec as P
 
 PAGE = 16
+EARLY = 3
 BLOCK = 128
 
 
-def attend_kernel(length_ref, q_ref, kv_ref, out_ref, k_ref, v_ref, *, blocks, heads):
+def attend_kernel(length_ref, q_ref, kv_ref, after_ref, out_ref, k_ref, v_ref, *, blocks, heads):
+    del after_ref
     head_dim = k_ref.shape[1]
     seq_len = k_ref.shape[0]
     step = pl.program_id(0)
@@ -54,7 +56,7 @@
         pl.when(step == index)(functools.partial(attend, index))
 
 
-def attend_local(queries, received, length, head_dim):
+def attend_local(queries, received, length, head_dim, after):
     seq_len, width = queries.shape
     heads = width // head_dim
     blocks = seq_len // BLOCK
@@ -65,6 +67,7 @@
             pl.BlockSpec(memory_space=pltpu.SMEM),
             pl.BlockSpec((BLOCK, width), lambda i: (i, 0)),
             pl.BlockSpec(received.shape, lambda i: (0, 0, 0, 0)),
+            pl.BlockSpec(memory_space=pl.ANY),
         ],
         out_specs=pl.BlockSpec((BLOCK, width), lambda i: (i, 0)),
         out_shape=jax.ShapeDtypeStruct((seq_len, width), jnp.bfloat16),
@@ -79,7 +82,7 @@
             transcendentals=seq_len * seq_len * heads,
         ),
         name="attend",
-    )(length, queries, received)
+    )(length, queries, received, after)
 
 
 def butterflies(values):
@@ -94,7 +97,8 @@
     return values
 
 
-def hadamard_kernel(in_ref, out_ref, mid_ref, *, heads):
+def hadamard_kernel(in_ref, after_ref, out_ref, mid_ref, *, heads):
+    del after_ref
     devices, tokens, width = in_ref.shape
     head_dim = width // heads
     factor = 1.0 / math.sqrt(devices * heads)
@@ -111,13 +115,13 @@
                 out_ref[device, rows, c] = (tile * factor).astype(jnp.bfloat16)
 
 
-def hadamard(blocks, heads):
+def hadamard(blocks, heads, after):
     devices, tokens, width = blocks.shape
     spec = pl.BlockSpec((devices, PAGE, width), lambda i: (0, i, 0))
     return pl.pallas_call(
         functools.partial(hadamard_kernel, heads=heads),
         grid=(tokens // PAGE,),
-        in_specs=[spec],
+        in_specs=[spec, pl.BlockSpec(memory_space=pl.ANY)],
         out_specs=spec,
         out_shape=jax.ShapeDtypeStruct(blocks.shape, jnp.bfloat16),
         scratch_shapes=[pltpu.VMEM((devices, PAGE, width), jnp.float32)],
@@ -126,42 +130,41 @@
             flops=7 * blocks.size, bytes_accessed=4 * blocks.size, transcendentals=0
         ),
         name="hadamard",
-    )(blocks)
+    )(blocks, after)
 
 
 def page_kernel(
-    length_ref, level_ref, side_ref, owner_ref, kv_ref, out_ref, count_ref, *, owners, capacity
+    length_ref, level_ref, side_ref, owner_ref, kv_ref, out_ref, count_ref, slot_ref, *, capacity
 ):
     sources, _, tokens, head_dim = kv_ref.shape
+    owners = out_ref.shape[0]
+    per_source = tokens // PAGE
     out_ref[...] = jnp.zeros_like(out_ref)
-    for owner in range(owners):
-        count_ref[owner] = 0
     level = level_ref[0].astype(jnp.float32)
     side = side_ref[0]
     rows = lax.broadcasted_iota(jnp.int32, (PAGE, head_dim), 0)
     tail = lax.broadcasted_iota(jnp.int32, (8, head_dim), 0)
-    per_source = tokens // PAGE
-
-    def one_page(page, _):
-        source = page // per_source
-        first = (page % per_source) * PAGE
-        values = kv_ref[source, side, pl.ds(pl.multiple_of(first, PAGE), PAGE), :]
-        live = page * PAGE + rows < length_ref[0]
-        values = jnp.where(live, values.astype(jnp.float32), 0.0)
+    for owner in range(owners):
+        count_ref[owner] = 0
+    for page in range(sources * per_source):
+        owner = owner_ref[page]
+        slot_ref[page] = jnp.minimum(count_ref[owner], capacity - 1)
+        count_ref[owner] = count_ref[owner] + 1
+
+    for page in range(sources * per_source):
+        part = page % per_source
+        values = kv_ref[page // per_source, side, part * PAGE : (part + 1) * PAGE, :]
+        values = jnp.where(page * PAGE + rows < length_ref[0], values.astype(jnp.float32), 0.0)
         total = jnp.sum(values * values, axis=(0, 1), keepdims=True)
         rms = jnp.sqrt(total / (PAGE * head_dim) + 1e-06)
         step = (rms * 0.5).astype(jnp.bfloat16).astype(jnp.float32)
         codes = jnp.clip(values / step, -level, level).astype(jnp.bfloat16)
         owner = owner_ref[page]
-        slot = jnp.minimum(count_ref[owner], capacity - 1)
-        count_ref[owner] = slot + 1
+        slot = slot_ref[page]
         out_ref[owner, pl.ds(pl.multiple_of(slot * PAGE, PAGE), PAGE), :] = codes
         before = out_ref[owner, capacity * PAGE :, :].astype(jnp.float32)
         steps = jnp.where(tail == slot, jnp.broadcast_to(step, tail.shape), before)
         out_ref[owner, capacity * PAGE :, :] = steps.astype(jnp.bfloat16)
-        return 0
-
-    lax.fori_loop(0, sources * per_source, one_page, 0)
 
 
 def page_table(received, length, level, owner_of, owners, capacity):
@@ -171,11 +174,14 @@
     side = (lax.axis_index("tp") % 2).astype(jnp.int32).reshape(1)
     shape = (owners, capacity * PAGE + 8, head_dim)
     return pl.pallas_call(
-        functools.partial(page_kernel, owners=owners, capacity=capacity),
+        functools.partial(page_kernel, capacity=capacity),
         in_specs=[smem, smem, smem, smem, vmem],
         out_specs=vmem,
         out_shape=jax.ShapeDtypeStruct(shape, jnp.bfloat16),
-        scratch_shapes=[pltpu.SMEM((owners,), jnp.int32)],
+        scratch_shapes=[
+            pltpu.SMEM((owners,), jnp.int32),
+            pltpu.SMEM(owner_of.shape, jnp.int32),
+        ],
         compiler_params=pltpu.CompilerParams(vmem_limit_bytes=32 * 1024 * 1024),
         cost_estimate=pl.CostEstimate(
             flops=10 * received.size, bytes_accessed=2 * received.size, transcendentals=0
@@ -184,17 +190,17 @@
     )(length, level, side, owner_of, received)
 
 
-def to_owners(table, axis):
+def to_owners(table, axis, bits, members):
     count = lax.axis_size(axis)
     position = lax.axis_index(axis)
     inner = table.shape[1:]
-    for bit in range(count.bit_length() - 1):
+    for bit in bits:
         stride = 1 << bit
         upper = jnp.right_shift(position, bit) % 2
         halves = table.reshape((count // (2 * stride), 2, stride) + inner)
         keep = lax.dynamic_index_in_dim(halves, upper, 1, keepdims=False)
         send = lax.dynamic_index_in_dim(halves, 1 - upper, 1, keepdims=False)
-        got = lax.ppermute(send, axis, [(i, i ^ stride) for i in range(count)])
+        got = lax.ppermute(send, axis, [(i, i ^ stride) for i in members])
         low = jnp.where(upper == 0, keep, got)
         high = jnp.where(upper == 0, got, keep)
         table = jnp.stack([low, high], axis=1).reshape((count,) + inner)
@@ -212,18 +218,31 @@
     seq_len = tp_count * tok_here
     heads_here = queries.shape[2] // head_dim
 
-    attended = attend_local(queries[0], received, lengths, head_dim)
-    blocks = attended.reshape(tp_count, seq_len // tp_count, heads_here * head_dim)
-    blocks = lax.all_to_all(blocks, "tp", split_axis=0, concat_axis=0, tiled=True)
-    mixed = hadamard(blocks, heads_here)
-    back = lax.all_to_all(mixed, "tp", split_axis=0, concat_axis=0, tiled=True)
-    rotated = back.reshape(1, seq_len, heads_here * head_dim)
-
     pages = seq_len // PAGE
     capacity = max(2, (3 * pages + 2 * owners - 1) // (2 * owners))
     level = 2 ** (bit_widths - 1) - 1
-    table = page_table(received, lengths, level, destinations[0, :, 0], owners, capacity)
-    table = to_owners(table, "req")
+    bits = list(range(1, owners.bit_length() - 1)) + [0]
+    first_bits, last_bits = bits[:EARLY], bits[EARLY:]
+    odd = lax.axis_index("req") % 2 == 1
+
+    def start_pages(members):
+        table = page_table(received, lengths, level, destinations[0, :, 0], owners, capacity)
+        return to_owners(table, "req", first_bits, members)
+
+    shape = (owners, capacity * PAGE + 8, head_dim)
+    table = lax.cond(
+        odd,
+        lambda: start_pages(range(1, owners, 2)),
+        lambda: jnp.zeros(shape, jnp.bfloat16),
+    )
+    attended = attend_local(queries[0], received, lengths, head_dim, table)
+    blocks = attended.reshape(tp_count, seq_len // tp_count, heads_here * head_dim)
+    blocks = lax.all_to_all(blocks, "tp", split_axis=0, concat_axis=0, tiled=True)
+    table = lax.cond(odd, lambda t: t, lambda t: start_pages(range(0, owners, 2)), table)
+    mixed = hadamard(blocks, heads_here, table)
+    back = lax.all_to_all(mixed, "tp", split_axis=0, concat_axis=0, tiled=True)
+    rotated = back.reshape(1, seq_len, heads_here * head_dim)
+    table = to_owners(table, "req", last_bits, range(owners))
     got_codes = table[:, : capacity * PAGE].reshape(1, owners, capacity, 1, PAGE, head_dim)
     got_steps = table[:, capacity * PAGE : capacity * (PAGE + 1), 0]
     return rotated, got_codes, got_steps.reshape(1, owners, capacity, 1)

time: 159 us -> 150 us (0.943)
  the two profiles are of different devices: /device:TPU:2 before, /device:TPU:1 now
where the time goes in v4:
time: 150 us
  waiting for transfers between devices  79 us (53%)
  starting transfers between devices  53.2 us (35%)
  Pallas kernels  8.93 us (6%)
  local copies, waits for them, and re-layouts  5.1 us (3%)
  between operations  2.12 us (1%)
    all_to_all x1, waiting for transfers between devices, body(): lax.all_to_all(blocks, 'tp', split_axis=0, concat_axis=0, tiled=True)  28.8 us
    all_to_all x1, waiting for transfers between devices, body(): back = lax.all_to_all(mixed, 'tp', split_axis=0, concat_axis=0, tiled=True)  25.4 us
    ppermute x5, starting transfers between devices, to_owners(): got = lax.ppermute(send, axis, [(i, i ^ stride) for i in members])  17.7 us
    all_to_all x1, starting transfers between devices, body(): lax.all_to_all(outgoing, 'tp', split_axis=0, concat_axis=0, tiled=True)  15.7 us
    ppermute x5, waiting for transfers between devices, to_owners(): got = lax.ppermute(send, axis, [(i, i ^ stride) for i in members])  13 us
    all_to_all x1, waiting for transfers between devices, body(): lax.all_to_all(outgoing, 'tp', split_axis=0, concat_axis=0, tiled=True)  11.8 us
    all_to_all x1, starting transfers between devices, body(): lax.all_to_all(blocks, 'tp', split_axis=0, concat_axis=0, tiled=True)  11.2 us
    all_to_all x1, starting transfers between devices, body(): back = lax.all_to_all(mixed, 'tp', split_axis=0, concat_axis=0, tiled=True)  8.54 us
  transfers between devices with their start and end apart: 8, of which 8 were waited for; matrix products, arithmetic and copies ran while one was open for 2% of the time, Pallas kernels for 0%

profile of v4, /device:TPU:1, one launch (start us, length us, event | category | flops | bytes accessed | tf_op | source)
XLA Modules:
  0.0 149.6 jit_solution(3350583703678026177)
XLA Ops:
  0.6 1.7 %broadcast_in_dim.7 = bf16[8,2,2,32,128]{4,3,2,1,0:T(8,128)(2,1)} broadcast(bf16[8,2,32,128]{3,2,1,0:T(8,128)(2,1)} %bitcast.160), dimensions={0,2,3,4} | broadcast | bytes 393216 | tf_op jit(solution)/shard_map/broadcast_in_dim | solution.py:216
  2.3 15.7 %all-to-all-start = ((bf16[16,2,32,128]{3,2,1,0:T(8,128)(2,1)}), bf16[16,2,32,128]{3,2,1,0:T(8,128)(2,1)S(1)}, u32[]{:S(2)}, u32[]{:S(2)}) async-start(bf16[16,2,32,128]{3,2,1,0:T(8,128)(2,1)} %bitcast.52), calls=%async_computation | async-start | bytes 524288 | tf_op jit(solution)/shard_map/all_to_all | solution.py:217
  19.4 0.0 copy-start.1
  19.4 11.8 %all-to-all-done.kv_ref = bf16[16,2,32,128]{3,2,1,0:T(8,128)(2,1)S(1)} async-done(((bf16[16,2,32,128]{3,2,1,0:T(8,128)(2,1)}), bf16[16,2,32,128]{3,2,1,0:T(8,128)(2,1)S(1)}, u32[]{:S(2)}, u32[]{:S(2)}) %all-to-all-start) | async-done | bytes 262176 | tf_op jit(solution)/shard_map/all_to_all | solution.py:217
  31.2 0.0 copy-done.1
  31.2 0.0 copy-start
  31.2 22.4 %conditional.2 = (bf16[32,40,128]{2,1,0:T(8,128)(2,1)}) conditional(s32[]{:T(128)} %convert_element_type.4, () %tuple.24, (s32[1,32,1]{1,2,0:T(1,128)S(1)}, s32[1]{0:T(128)}, s32[1]{0:T(128)}, bf16[16,2,32,128]{3,2,1,0:T(8,128)(2,1)S(1)}) %tuple.43), branch_computations={%region_0.1_spmd, %region_1.2_spmd} | conditional | flops 2293836 | bytes 7144370 | solution.py:233
  31.2 1.6 %pages.2 = bf16[32,40,128]{2,1,0:T(8,128)(2,1)S(1)} custom-call(s32[1]{0:T(128)} %get-tuple-element.23.length_ref, s32[1]{0:T(128)} %get-tuple-element.24.level_ref, s32[1]{0:T(128)} %bitcast.side_ref, s32[32]{0:T(128)S(1)} %bitcast.161, bf16[16,2,32,128]{3,2,1,0:T(8,128)(2,1)S(1)} %get-tuple-element.26.kv_ref), custom_call_target="tpu_custom_call" | custom-call | flops 1310720 | bytes 262144 | tf_op jit(solution)/shard_map/cond/branch_1_fun/pages/pallas_call | solution.py:176
  32.9 3.1 %collective-permute-start = (bf16[8,2,40,128]{3,2,1,0:T(8,128)(2,1)S(1)}, bf16[8,2,40,128]{3,2,1,0:T(8,128)(2,1)S(1)}, u32[]{:S(2)}, u32[]{:S(2)}) collective-permute-start(bf16[8,2,40,128]{3,2,1,0:T(8,128)(2,1)S(1)} %dynamic-slice_bitcast_fusion.2), channel_id=1, source_target_pairs={{16,48},{48,16},{80,112},{112,80},{144,176},{176,144},{208,240},{2... | collective-permute-start | bytes 491528 | tf_op jit(solution)/shard_map/cond/branch_1_fun/ppermute | solution.py:203
  36.0 2.9 %collective-permute-done = bf16[8,2,40,128]{3,2,1,0:T(8,128)(2,1)S(1)} collective-permute-done((bf16[8,2,40,128]{3,2,1,0:T(8,128)(2,1)S(1)}, bf16[8,2,40,128]{3,2,1,0:T(8,128)(2,1)S(1)}, u32[]{:S(2)}, u32[]{:S(2)}) %collective-permute-start) | collective-permute-done | bytes 163872 | tf_op jit(solution)/shard_map/cond/branch_1_fun/ppermute | solution.py:203
  39.0 4.7 %collective-permute-start.1 = (bf16[4,4,40,128]{3,2,1,0:T(8,128)(2,1)S(1)}, bf16[4,4,40,128]{3,2,1,0:T(8,128)(2,1)S(1)}, u32[]{:S(2)}, u32[]{:S(2)}) collective-permute-start(bf16[4,4,40,128]{3,2,1,0:T(8,128)(2,1)S(1)} %dynamic-slice_bitcast_fusion.1), channel_id=1, source_target_pairs={{16,80},{48,112},{80,16},{112,48},{144,208},{176,240},{208,144},{2... | collective-permute-start | bytes 491528 | tf_op jit(solution)/shard_map/cond/branch_1_fun/ppermute | solution.py:203
  43.7 2.9 %collective-permute-done.1 = bf16[4,4,40,128]{3,2,1,0:T(8,128)(2,1)S(1)} collective-permute-done((bf16[4,4,40,128]{3,2,1,0:T(8,128)(2,1)S(1)}, bf16[4,4,40,128]{3,2,1,0:T(8,128)(2,1)S(1)}, u32[]{:S(2)}, u32[]{:S(2)}) %collective-permute-start.1) | collective-permute-done | bytes 163872 | tf_op jit(solution)/shard_map/cond/branch_1_fun/ppermute | solution.py:203
  46.7 3.2 %collective-permute-start.2 = (bf16[2,8,40,128]{3,2,1,0:T(8,128)(2,1)S(1)}, bf16[2,8,40,128]{3,2,1,0:T(8,128)(2,1)S(1)}, u32[]{:S(2)}, u32[]{:S(2)}) collective-permute-start(bf16[2,8,40,128]{3,2,1,0:T(8,128)(2,1)S(1)} %dynamic-slice_bitcast_fusion), channel_id=1, source_target_pairs={{16,144},{48,176},{80,208},{112,240},{144,16},{176,48},{208,80},{2... | collective-permute-start | bytes 491528 | tf_op jit(solution)/shard_map/cond/branch_1_fun/ppermute | solution.py:203
  49.9 2.8 %collective-permute-done.2 = bf16[2,8,40,128]{3,2,1,0:T(8,128)(2,1)S(1)} collective-permute-done((bf16[2,8,40,128]{3,2,1,0:T(8,128)(2,1)S(1)}, bf16[2,8,40,128]{3,2,1,0:T(8,128)(2,1)S(1)}, u32[]{:S(2)}, u32[]{:S(2)}) %collective-permute-start.2) | collective-permute-done | bytes 163872 | tf_op jit(solution)/shard_map/cond/branch_1_fun/ppermute | solution.py:203
  52.8 0.8 pad_maximum_fusion.2
  53.5 0.0 copy-done
  53.6 5.5 %attend.1 = bf16[512,1024]{1,0:T(8,128)(2,1)} custom-call(s32[1]{0:T(128)S(6)} %copy.40.length_ref, bf16[512,1024]{1,0:T(8,128)(2,1)S(1)} %bitcast.145, bf16[16,2,32,128]{3,2,1,0:T(8,128)(2,1)S(1)} %all-to-all-done.kv_ref, bf16[32,40,128]{2,1,0:T(8,128)(2,1)} %get-tuple-element.70.after_ref), custom_call_target="tpu_custom_call" | custom-call | flops 1073741824 | bytes 2097152 | tf_op jit(solution)/shard_map/attend/pallas_call | solution.py:63
  59.1 11.2 %all-to-all-start.1 = ((bf16[16,32,1024]{2,1,0:T(8,128)(2,1)}), bf16[16,32,1024]{2,1,0:T(8,128)(2,1)S(1)}, u32[]{:S(2)}, u32[]{:S(2)}) async-start(bf16[16,32,1024]{2,1,0:T(8,128)(2,1)} %bitcast.53), calls=%async_computation.1 | async-start | bytes 2097152 | tf_op jit(solution)/shard_map/all_to_all | solution.py:240
  70.3 1.0 conditional.3
  70.3 1.0 copy.37
  71.3 28.8 %all-to-all-done.1.in_ref = bf16[16,32,1024]{2,1,0:T(8,128)(2,1)S(1)} async-done(((bf16[16,32,1024]{2,1,0:T(8,128)(2,1)}), bf16[16,32,1024]{2,1,0:T(8,128)(2,1)S(1)}, u32[]{:S(2)}, u32[]{:S(2)}) %all-to-all-start.1) | async-done | bytes 1048608 | tf_op jit(solution)/shard_map/all_to_all | solution.py:240
  100.1 1.8 %hadamard.1 = bf16[16,32,1024]{2,1,0:T(8,128)(2,1)} custom-call(bf16[16,32,1024]{2,1,0:T(8,128)(2,1)S(1)} %all-to-all-done.1.in_ref, bf16[32,40,128]{2,1,0:T(8,128)(2,1)} %get-tuple-element.36.after_ref), custom_call_target="tpu_custom_call" | custom-call | flops 3670016 | bytes 2097152 | tf_op jit(solution)/shard_map/hadamard/pallas_call | solution.py:121
  101.9 8.5 %all-to-all-start.2 = ((bf16[16,32,1024]{2,1,0:T(8,128)(2,1)}), bf16[16,32,1024]{2,1,0:T(8,128)(2,1)S(1)}, u32[]{:S(2)}, u32[]{:S(2)}) async-start(bf16[16,32,1024]{2,1,0:T(8,128)(2,1)} %hadamard.1), calls=%async_computation.2 | async-start | bytes 2097152 | tf_op jit(solution)/shard_map/all_to_all | solution.py:243
  110.4 4.8 %collective-permute-start.6 = (bf16[1,16,40,128]{3,2,1,0:T(8,128)(2,1)S(1)}, bf16[1,16,40,128]{3,2,1,0:T(8,128)(2,1)S(1)}, u32[]{:S(2)}, u32[]{:S(2)}) collective-permute-start(bf16[1,16,40,128]{3,2,1,0:T(8,128)(2,1)S(1)} %dynamic-slice_bitcast_fusion.7), channel_id=1, source_target_pairs={{0,256},{16,272},{32,288},{48,304},{64,320},{80,336},{96,352},{112... | collective-permute-start | bytes 491528 | tf_op jit(solution)/shard_map/ppermute | solution.py:203
  115.3 3.0 %collective-permute-done.6 = bf16[1,16,40,128]{3,2,1,0:T(8,128)(2,1)S(1)} collective-permute-done((bf16[1,16,40,128]{3,2,1,0:T(8,128)(2,1)S(1)}, bf16[1,16,40,128]{3,2,1,0:T(8,128)(2,1)S(1)}, u32[]{:S(2)}, u32[]{:S(2)}) %collective-permute-start.6) | collective-permute-done | bytes 163872 | tf_op jit(solution)/shard_map/ppermute | solution.py:203
  118.4 1.9 %collective-permute-start.7 = (bf16[16,1,40,128]{3,2,0,1:T(8,128)(2,1)S(1)}, bf16[16,1,40,128]{3,2,0,1:T(8,128)(2,1)S(1)}, u32[]{:S(2)}, u32[]{:S(2)}) collective-permute-start(bf16[16,1,40,128]{3,2,0,1:T(8,128)(2,1)S(1)} %dynamic-slice_bitcast_fusion.6), channel_id=1, source_target_pairs={{0,16},{16,0},{32,48},{48,32},{64,80},{80,64},{96,112},{112,96},{1... | collective-permute-start | bytes 491528 | tf_op jit(solution)/shard_map/ppermute | solution.py:203
  120.3 1.4 collective-permute-done.7
  121.8 0.7 slice.8
  122.6 0.6 copy.30
  123.2 25.4 %all-to-all-done.2 = bf16[16,32,1024]{2,1,0:T(8,128)(2,1)S(1)} async-done(((bf16[16,32,1024]{2,1,0:T(8,128)(2,1)}), bf16[16,32,1024]{2,1,0:T(8,128)(2,1)S(1)}, u32[]{:S(2)}, u32[]{:S(2)}) %all-to-all-start.2) | async-done | bytes 1048608 | tf_op jit(solution)/shard_map/all_to_all | solution.py:243
  148.6 1.0 copy.41
  (16 shorter events, 0.4 us)
Async XLA Ops:
  2.3 28.9 %all-to-all-start = ((bf16[16,2,32,128]{3,2,1,0:T(8,128)(2,1)}), bf16[16,2,32,128]{3,2,1,0:T(8,128)(2,1)S(1)}, u32[]{:S(2)}, u32[]{:S(2)}) async-start(bf16[16,2,32,128]{3,2,1,0:T(8,128)(2,1)} %bitcast.52), calls=%async_computation | async-start | bytes 524288 | tf_op jit(solution)/shard_map/all_to_all | solution.py:217
  19.4 11.8 %copy-start.1 = (s32[1,32,1]{1,2,0:T(1,128)S(1)}, s32[1,32,1]{1,2,0:T(1,128)}, u32[]{:S(2)}) copy-start(s32[1,32,1]{1,2,0:T(1,128)} %param.12) | copy-start | bytes 388
  31.2 22.4 %copy-start = (bf16[1,512,1024]{2,1,0:T(8,128)(2,1)S(1)}, bf16[1,512,1024]{2,1,0:T(8,128)(2,1)}, u32[]{:S(2)}) copy-start(bf16[1,512,1024]{2,1,0:T(8,128)(2,1)} %param.9) | copy-start | bytes 3145732
  32.9 6.1 %collective-permute-start = (bf16[8,2,40,128]{3,2,1,0:T(8,128)(2,1)S(1)}, bf16[8,2,40,128]{3,2,1,0:T(8,128)(2,1)S(1)}, u32[]{:S(2)}, u32[]{:S(2)}) collective-permute-start(bf16[8,2,40,128]{3,2,1,0:T(8,128)(2,1)S(1)} %dynamic-slice_bitcast_fusion.2), channel_id=1, source_target_pairs={{16,48},{48,16},{80,112},{112,80},{144,176},{176,144},{208,240},{2... | collective-permute-start | bytes 491528 | tf_op jit(solution)/shard_map/cond/branch_1_fun/ppermute | solution.py:203
  39.0 7.6 %collective-permute-start.1 = (bf16[4,4,40,128]{3,2,1,0:T(8,128)(2,1)S(1)}, bf16[4,4,40,128]{3,2,1,0:T(8,128)(2,1)S(1)}, u32[]{:S(2)}, u32[]{:S(2)}) collective-permute-start(bf16[4,4,40,128]{3,2,1,0:T(8,128)(2,1)S(1)} %dynamic-slice_bitcast_fusion.1), channel_id=1, source_target_pairs={{16,80},{48,112},{80,16},{112,48},{144,208},{176,240},{208,144},{2... | collective-permute-start | bytes 491528 | tf_op jit(solution)/shard_map/cond/branch_1_fun/ppermute | solution.py:203
  46.7 6.1 %collective-permute-start.2 = (bf16[2,8,40,128]{3,2,1,0:T(8,128)(2,1)S(1)}, bf16[2,8,40,128]{3,2,1,0:T(8,128)(2,1)S(1)}, u32[]{:S(2)}, u32[]{:S(2)}) collective-permute-start(bf16[2,8,40,128]{3,2,1,0:T(8,128)(2,1)S(1)} %dynamic-slice_bitcast_fusion), channel_id=1, source_target_pairs={{16,144},{48,176},{80,208},{112,240},{144,16},{176,48},{208,80},{2... | collective-permute-start | bytes 491528 | tf_op jit(solution)/shard_map/cond/branch_1_fun/ppermute | solution.py:203
  59.1 41.0 %all-to-all-start.1 = ((bf16[16,32,1024]{2,1,0:T(8,128)(2,1)}), bf16[16,32,1024]{2,1,0:T(8,128)(2,1)S(1)}, u32[]{:S(2)}, u32[]{:S(2)}) async-start(bf16[16,32,1024]{2,1,0:T(8,128)(2,1)} %bitcast.53), calls=%async_computation.1 | async-start | bytes 2097152 | tf_op jit(solution)/shard_map/all_to_all | solution.py:240
  101.9 46.7 %all-to-all-start.2 = ((bf16[16,32,1024]{2,1,0:T(8,128)(2,1)}), bf16[16,32,1024]{2,1,0:T(8,128)(2,1)S(1)}, u32[]{:S(2)}, u32[]{:S(2)}) async-start(bf16[16,32,1024]{2,1,0:T(8,128)(2,1)} %hadamard.1), calls=%async_computation.2 | async-start | bytes 2097152 | tf_op jit(solution)/shard_map/all_to_all | solution.py:243
  110.4 7.9 %collective-permute-start.6 = (bf16[1,16,40,128]{3,2,1,0:T(8,128)(2,1)S(1)}, bf16[1,16,40,128]{3,2,1,0:T(8,128)(2,1)S(1)}, u32[]{:S(2)}, u32[]{:S(2)}) collective-permute-start(bf16[1,16,40,128]{3,2,1,0:T(8,128)(2,1)S(1)} %dynamic-slice_bitcast_fusion.7), channel_id=1, source_target_pairs={{0,256},{16,272},{32,288},{48,304},{64,320},{80,336},{96,352},{112... | collective-permute-start | bytes 491528 | tf_op jit(solution)/shard_map/ppermute | solution.py:203
  118.4 3.3 %collective-permute-start.7 = (bf16[16,1,40,128]{3,2,0,1:T(8,128)(2,1)S(1)}, bf16[16,1,40,128]{3,2,0,1:T(8,128)(2,1)S(1)}, u32[]{:S(2)}, u32[]{:S(2)}) collective-permute-start(bf16[16,1,40,128]{3,2,0,1:T(8,128)(2,1)S(1)} %dynamic-slice_bitcast_fusion.6), channel_id=1, source_target_pairs={{0,16},{16,0},{32,48},{48,32},{64,80},{80,64},{96,112},{112,96},{1... | collective-permute-start | bytes 491528 | tf_op jit(solution)/shard_map/ppermute | solution.py:203

commit v5 on v4

--- a/solution.py
+++ b/solution.py
@@ -10,72 +10,77 @@
 
 PAGE = 16
 EARLY = 3
-BLOCK = 128
-
-
-def attend_kernel(length_ref, q_ref, kv_ref, after_ref, out_ref, k_ref, v_ref, *, blocks, heads):
+SMEM = pl.BlockSpec(memory_space=pltpu.SMEM)
+VMEM = pl.BlockSpec(memory_space=pltpu.VMEM)
+ANYWHERE = pl.BlockSpec(memory_space=pl.ANY)
+BLOCK = 256
+
+
+def attend_kernel(
+    length_ref, q_hbm, kv_ref, after_ref, out_hbm, q_ref, out_ref, sems, k_ref, v_ref, *, heads
+):
     del after_ref
-    head_dim = k_ref.shape[1]
-    seq_len = k_ref.shape[0]
-    step = pl.program_id(0)
-
-    @pl.when(step == 0)
-    def _():
-        k_ref[...] = kv_ref[:, 0].reshape(seq_len, head_dim)
-        v_ref[:, :head_dim] = kv_ref[:, 1].reshape(seq_len, head_dim)
-        v_ref[:, head_dim:] = jnp.ones((seq_len, head_dim), jnp.bfloat16)
-
+    seq_len, head_dim = k_ref.shape
+    parts = [slice(first, first + BLOCK) for first in range(0, seq_len, BLOCK)]
+    fetches = [
+        pltpu.make_async_copy(q_hbm.at[part], q_ref.at[part], sems.at[0, index])
+        for index, part in enumerate(parts)
+    ]
+    writes = [
+        pltpu.make_async_copy(out_ref.at[part], out_hbm.at[part], sems.at[1, index])
+        for index, part in enumerate(parts)
+    ]
+    for fetch in fetches:
+        fetch.start()
+    k_ref[...] = kv_ref[:, 0].reshape(seq_len, head_dim)
+    v_ref[:, :head_dim] = kv_ref[:, 1].reshape(seq_len, head_dim)
+    v_ref[:, head_dim:] = jnp.ones((seq_len, head_dim), jnp.bfloat16)
     rate = math.log2(math.e) / math.sqrt(head_dim)
     rows = lax.broadcasted_iota(jnp.int32, (BLOCK, BLOCK), 0)
     cols = lax.broadcasted_iota(jnp.int32, (BLOCK, BLOCK), 1)
     causal = rows >= cols
-    live = step * BLOCK + lax.broadcasted_iota(jnp.int32, (BLOCK, head_dim), 0) < length_ref[0]
-
-    def attend(index):
-        finish = (index + 1) * BLOCK
-        for head in range(heads):
-            columns = slice(head * head_dim, (head + 1) * head_dim)
+    row = lax.broadcasted_iota(jnp.int32, (BLOCK, head_dim), 0)
+
+    for index, part in enumerate(parts):
+        fetches[index].wait()
+        start, finish = part.start, part.stop
+        live = row + start < length_ref[0]
+        for column in range(0, heads * head_dim, head_dim):
+            columns = slice(column, column + head_dim)
             scores = lax.dot_general(
-                q_ref[:, columns],
+                q_ref[part, columns],
                 k_ref[:finish],
                 (((1,), (1,)), ((), ())),
                 preferred_element_type=jnp.float32,
             )
-            last = jnp.where(causal, scores[:, index * BLOCK :], -jnp.inf)
-            if index:
-                scores = jnp.concatenate([scores[:, : index * BLOCK], last], axis=1)
-            else:
-                scores = last
+            last = jnp.where(causal, scores[:, start:], -jnp.inf)
+            scores = jnp.concatenate([scores[:, :start], last], axis=1) if start else last
             top = jnp.max(scores, axis=1, keepdims=True)
             weights = jnp.exp2((scores - top) * rate).astype(jnp.bfloat16)
             both = jnp.dot(weights, v_ref[:finish], preferred_element_type=jnp.float32)
             attended = both[:, :head_dim] / both[:, head_dim:]
-            out_ref[:, columns] = jnp.where(live, attended, 0.0).astype(jnp.bfloat16)
-
-    for index in range(blocks):
-        pl.when(step == index)(functools.partial(attend, index))
+            out_ref[part, columns] = jnp.where(live, attended, 0.0).astype(jnp.bfloat16)
+        writes[index].start()
+    for write in writes:
+        write.wait()
 
 
 def attend_local(queries, received, length, head_dim, after):
     seq_len, width = queries.shape
     heads = width // head_dim
-    blocks = seq_len // BLOCK
-    return pl.pallas_call(
-        functools.partial(attend_kernel, blocks=blocks, heads=heads),
-        grid=(blocks,),
-        in_specs=[
-            pl.BlockSpec(memory_space=pltpu.SMEM),
-            pl.BlockSpec((BLOCK, width), lambda i: (i, 0)),
-            pl.BlockSpec(received.shape, lambda i: (0, 0, 0, 0)),
-            pl.BlockSpec(memory_space=pl.ANY),
-        ],
-        out_specs=pl.BlockSpec((BLOCK, width), lambda i: (i, 0)),
+    return pl.pallas_call(
+        functools.partial(attend_kernel, heads=heads),
+        in_specs=[SMEM, ANYWHERE, VMEM, ANYWHERE],
+        out_specs=ANYWHERE,
         out_shape=jax.ShapeDtypeStruct((seq_len, width), jnp.bfloat16),
         scratch_shapes=[
+            pltpu.VMEM((seq_len, width), jnp.bfloat16),
+            pltpu.VMEM((seq_len, width), jnp.bfloat16),
+            pltpu.SemaphoreType.DMA((2, seq_len // BLOCK)),
             pltpu.VMEM((seq_len, head_dim), jnp.bfloat16),
             pltpu.VMEM((seq_len, 2 * head_dim), jnp.bfloat16),
         ],
-        compiler_params=pltpu.CompilerParams(vmem_limit_bytes=32 * 1024 * 1024),
+        compiler_params=pltpu.CompilerParams(vmem_limit_bytes=62 * 1024 * 1024),
         cost_estimate=pl.CostEstimate(
             flops=4 * seq_len * seq_len * width,
             bytes_accessed=4 * seq_len * width,
@@ -83,6 +88,18 @@
         ),
         name="attend",
     )(length, queries, received, after)
+
+
+def placeholder(shape):
+    def nothing(out_ref):
+        del out_ref
+
+    return pl.pallas_call(
+        nothing,
+        out_specs=pl.BlockSpec(memory_space=pl.ANY),
+        out_shape=jax.ShapeDtypeStruct(shape, jnp.bfloat16),
+        name="placeholder",
+    )()
 
 
 def butterflies(values):
@@ -233,7 +250,7 @@
     table = lax.cond(
         odd,
         lambda: start_pages(range(1, owners, 2)),
-        lambda: jnp.zeros(shape, jnp.bfloat16),
+        lambda: placeholder(shape),
     )
     attended = attend_local(queries[0], received, lengths, head_dim, table)
     blocks = attended.reshape(tp_count, seq_len // tp_count, heads_here * head_dim)

time: 150 us -> 147 us (0.980)
  no operation moved by 1% of the time
where the time goes in v5:
time: 147 us
  waiting for transfers between devices  78.3 us (53%)
  starting transfers between devices  52.2 us (36%)
  Pallas kernels  7.66 us (5%)
  local copies, waits for them, and re-layouts  5.09 us (3%)
  between operations  2.12 us (1%)
    all_to_all x1, waiting for transfers between devices, body(): lax.all_to_all(blocks, 'tp', split_axis=0, concat_axis=0, tiled=True)  28.6 us
    all_to_all x1, waiting for transfers between devices, body(): back = lax.all_to_all(mixed, 'tp', split_axis=0, concat_axis=0, tiled=True)  25 us
    ppermute x5, starting transfers between devices, to_owners(): got = lax.ppermute(send, axis, [(i, i ^ stride) for i in members])  17.7 us
    all_to_all x1, starting transfers between devices, body(): lax.all_to_all(outgoing, 'tp', split_axis=0, concat_axis=0, tiled=True)  15.7 us
    ppermute x5, waiting for transfers between devices, to_owners(): got = lax.ppermute(send, axis, [(i, i ^ stride) for i in members])  13 us
    all_to_all x1, waiting for transfers between devices, body(): lax.all_to_all(outgoing, 'tp', split_axis=0, concat_axis=0, tiled=True)  11.8 us
    all_to_all x1, starting transfers between devices, body(): lax.all_to_all(blocks, 'tp', split_axis=0, concat_axis=0, tiled=True)  11.3 us
    all_to_all x1, starting transfers between devices, body(): back = lax.all_to_all(mixed, 'tp', split_axis=0, concat_axis=0, tiled=True)  7.5 us
  transfers between devices with their start and end apart: 8, of which 8 were waited for; matrix products, arithmetic and copies ran while one was open for 2% of the time, Pallas kernels for 0%

profile of v5, /device:TPU:1, one launch (start us, length us, event | category | flops | bytes accessed | tf_op | source)
XLA Modules:
  0.0 146.6 jit_solution(2418124093983337606)
XLA Ops:
  0.6 1.7 %broadcast_in_dim.7 = bf16[8,2,2,32,128]{4,3,2,1,0:T(8,128)(2,1)} broadcast(bf16[8,2,32,128]{3,2,1,0:T(8,128)(2,1)} %bitcast.160), dimensions={0,2,3,4} | broadcast | bytes 393216 | tf_op jit(solution)/shard_map/broadcast_in_dim | solution.py:233
  2.3 15.7 %all-to-all-start = ((bf16[16,2,32,128]{3,2,1,0:T(8,128)(2,1)}), bf16[16,2,32,128]{3,2,1,0:T(8,128)(2,1)S(1)}, u32[]{:S(2)}, u32[]{:S(2)}) async-start(bf16[16,2,32,128]{3,2,1,0:T(8,128)(2,1)} %bitcast.52), calls=%async_computation | async-start | bytes 524288 | tf_op jit(solution)/shard_map/all_to_all | solution.py:234
  19.4 0.0 copy-start
  19.4 11.8 %all-to-all-done.kv_ref = bf16[16,2,32,128]{3,2,1,0:T(8,128)(2,1)S(1)} async-done(((bf16[16,2,32,128]{3,2,1,0:T(8,128)(2,1)}), bf16[16,2,32,128]{3,2,1,0:T(8,128)(2,1)S(1)}, u32[]{:S(2)}, u32[]{:S(2)}) %all-to-all-start) | async-done | bytes 262176 | tf_op jit(solution)/shard_map/all_to_all | solution.py:234
  31.2 0.0 copy-done
  31.2 22.3 %conditional.2 = (bf16[32,40,128]{2,1,0:T(8,128)(2,1)}) conditional(s32[]{:T(128)} %convert_element_type.4, () %tuple.24, (s32[1,32,1]{1,2,0:T(1,128)S(1)}, s32[1]{0:T(128)}, s32[1]{0:T(128)}, bf16[16,2,32,128]{3,2,1,0:T(8,128)(2,1)S(1)}) %tuple.43), branch_computations={%region_0.1_spmd, %region_1.2_spmd} | conditional | flops 2293836 | bytes 7144370 | solution.py:250
  31.2 1.6 %pages.2 = bf16[32,40,128]{2,1,0:T(8,128)(2,1)S(1)} custom-call(s32[1]{0:T(128)} %get-tuple-element.23.length_ref, s32[1]{0:T(128)} %get-tuple-element.24.level_ref, s32[1]{0:T(128)} %bitcast.side_ref, s32[32]{0:T(128)S(1)} %bitcast.161, bf16[16,2,32,128]{3,2,1,0:T(8,128)(2,1)S(1)} %get-tuple-element.26.kv_ref), custom_call_target="tpu_custom_call" | custom-call | flops 1310720 | bytes 262144 | tf_op jit(solution)/shard_map/cond/branch_1_fun/pages/pallas_call | solution.py:193
  32.8 3.1 %collective-permute-start = (bf16[8,2,40,128]{3,2,1,0:T(8,128)(2,1)S(1)}, bf16[8,2,40,128]{3,2,1,0:T(8,128)(2,1)S(1)}, u32[]{:S(2)}, u32[]{:S(2)}) collective-permute-start(bf16[8,2,40,128]{3,2,1,0:T(8,128)(2,1)S(1)} %dynamic-slice_bitcast_fusion.2), channel_id=1, source_target_pairs={{16,48},{48,16},{80,112},{112,80},{144,176},{176,144},{208,240},{2... | collective-permute-start | bytes 491528 | tf_op jit(solution)/shard_map/cond/branch_1_fun/ppermute | solution.py:220
  35.9 2.9 %collective-permute-done = bf16[8,2,40,128]{3,2,1,0:T(8,128)(2,1)S(1)} collective-permute-done((bf16[8,2,40,128]{3,2,1,0:T(8,128)(2,1)S(1)}, bf16[8,2,40,128]{3,2,1,0:T(8,128)(2,1)S(1)}, u32[]{:S(2)}, u32[]{:S(2)}) %collective-permute-start) | collective-permute-done | bytes 163872 | tf_op jit(solution)/shard_map/cond/branch_1_fun/ppermute | solution.py:220
  38.9 4.7 %collective-permute-start.1 = (bf16[4,4,40,128]{3,2,1,0:T(8,128)(2,1)S(1)}, bf16[4,4,40,128]{3,2,1,0:T(8,128)(2,1)S(1)}, u32[]{:S(2)}, u32[]{:S(2)}) collective-permute-start(bf16[4,4,40,128]{3,2,1,0:T(8,128)(2,1)S(1)} %dynamic-slice_bitcast_fusion.1), channel_id=1, source_target_pairs={{16,80},{48,112},{80,16},{112,48},{144,208},{176,240},{208,144},{2... | collective-permute-start | bytes 491528 | tf_op jit(solution)/shard_map/cond/branch_1_fun/ppermute | solution.py:220
  43.6 2.9 %collective-permute-done.1 = bf16[4,4,40,128]{3,2,1,0:T(8,128)(2,1)S(1)} collective-permute-done((bf16[4,4,40,128]{3,2,1,0:T(8,128)(2,1)S(1)}, bf16[4,4,40,128]{3,2,1,0:T(8,128)(2,1)S(1)}, u32[]{:S(2)}, u32[]{:S(2)}) %collective-permute-start.1) | collective-permute-done | bytes 163872 | tf_op jit(solution)/shard_map/cond/branch_1_fun/ppermute | solution.py:220
  46.6 3.2 %collective-permute-start.2 = (bf16[2,8,40,128]{3,2,1,0:T(8,128)(2,1)S(1)}, bf16[2,8,40,128]{3,2,1,0:T(8,128)(2,1)S(1)}, u32[]{:S(2)}, u32[]{:S(2)}) collective-permute-start(bf16[2,8,40,128]{3,2,1,0:T(8,128)(2,1)S(1)} %dynamic-slice_bitcast_fusion), channel_id=1, source_target_pairs={{16,144},{48,176},{80,208},{112,240},{144,16},{176,48},{208,80},{2... | collective-permute-start | bytes 491528 | tf_op jit(solution)/shard_map/cond/branch_1_fun/ppermute | solution.py:220
  49.8 2.8 %collective-permute-done.2 = bf16[2,8,40,128]{3,2,1,0:T(8,128)(2,1)S(1)} collective-permute-done((bf16[2,8,40,128]{3,2,1,0:T(8,128)(2,1)S(1)}, bf16[2,8,40,128]{3,2,1,0:T(8,128)(2,1)S(1)}, u32[]{:S(2)}, u32[]{:S(2)}) %collective-permute-start.2) | collective-permute-done | bytes 163872 | tf_op jit(solution)/shard_map/cond/branch_1_fun/ppermute | solution.py:220
  52.7 0.8 pad_maximum_fusion.2
  53.5 4.3 %attend.1 = bf16[512,1024]{1,0:T(8,128)(2,1)} custom-call(s32[1]{0:T(128)S(6)} %copy.40.length_ref, bf16[512,1024]{1,0:T(8,128)(2,1)} %bitcast.164, bf16[16,2,32,128]{3,2,1,0:T(8,128)(2,1)S(1)} %all-to-all-done.kv_ref, bf16[32,40,128]{2,1,0:T(8,128)(2,1)} %get-tuple-element.70.after_ref), custom_call_target="tpu_custom_call" | custom-call | flops 1073741824 | bytes 2097152 | tf_op jit(solution)/shard_map/attend/pallas_call | solution.py:71
  57.8 11.3 %all-to-all-start.1 = ((bf16[16,32,1024]{2,1,0:T(8,128)(2,1)}), bf16[16,32,1024]{2,1,0:T(8,128)(2,1)S(1)}, u32[]{:S(2)}, u32[]{:S(2)}) async-start(bf16[16,32,1024]{2,1,0:T(8,128)(2,1)} %bitcast.158), calls=%async_computation.1 | async-start | bytes 2097152 | tf_op jit(solution)/shard_map/all_to_all | solution.py:257
  69.0 1.0 conditional.3
  69.1 1.0 copy.37
  70.0 28.6 %all-to-all-done.1.in_ref = bf16[16,32,1024]{2,1,0:T(8,128)(2,1)S(1)} async-done(((bf16[16,32,1024]{2,1,0:T(8,128)(2,1)}), bf16[16,32,1024]{2,1,0:T(8,128)(2,1)S(1)}, u32[]{:S(2)}, u32[]{:S(2)}) %all-to-all-start.1) | async-done | bytes 1048608 | tf_op jit(solution)/shard_map/all_to_all | solution.py:257
  98.6 1.8 %hadamard.1 = bf16[16,32,1024]{2,1,0:T(8,128)(2,1)} custom-call(bf16[16,32,1024]{2,1,0:T(8,128)(2,1)S(1)} %all-to-all-done.1.in_ref, bf16[32,40,128]{2,1,0:T(8,128)(2,1)} %get-tuple-element.36.after_ref), custom_call_target="tpu_custom_call" | custom-call | flops 3670016 | bytes 2097152 | tf_op jit(solution)/shard_map/hadamard/pallas_call | solution.py:138
  100.4 7.5 %all-to-all-start.2 = ((bf16[16,32,1024]{2,1,0:T(8,128)(2,1)}), bf16[16,32,1024]{2,1,0:T(8,128)(2,1)S(1)}, u32[]{:S(2)}, u32[]{:S(2)}) async-start(bf16[16,32,1024]{2,1,0:T(8,128)(2,1)} %hadamard.1), calls=%async_computation.2 | async-start | bytes 2097152 | tf_op jit(solution)/shard_map/all_to_all | solution.py:260
  107.9 4.8 %collective-permute-start.6 = (bf16[1,16,40,128]{3,2,1,0:T(8,128)(2,1)S(1)}, bf16[1,16,40,128]{3,2,1,0:T(8,128)(2,1)S(1)}, u32[]{:S(2)}, u32[]{:S(2)}) collective-permute-start(bf16[1,16,40,128]{3,2,1,0:T(8,128)(2,1)S(1)} %dynamic-slice_bitcast_fusion.7), channel_id=1, source_target_pairs={{0,256},{16,272},{32,288},{48,304},{64,320},{80,336},{96,352},{112... | collective-permute-start | bytes 491528 | tf_op jit(solution)/shard_map/ppermute | solution.py:220
  112.8 3.0 %collective-permute-done.6 = bf16[1,16,40,128]{3,2,1,0:T(8,128)(2,1)S(1)} collective-permute-done((bf16[1,16,40,128]{3,2,1,0:T(8,128)(2,1)S(1)}, bf16[1,16,40,128]{3,2,1,0:T(8,128)(2,1)S(1)}, u32[]{:S(2)}, u32[]{:S(2)}) %collective-permute-start.6) | collective-permute-done | bytes 163872 | tf_op jit(solution)/shard_map/ppermute | solution.py:220
  115.9 1.9 %collective-permute-start.7 = (bf16[16,1,40,128]{3,2,0,1:T(8,128)(2,1)S(1)}, bf16[16,1,40,128]{3,2,0,1:T(8,128)(2,1)S(1)}, u32[]{:S(2)}, u32[]{:S(2)}) collective-permute-start(bf16[16,1,40,128]{3,2,0,1:T(8,128)(2,1)S(1)} %dynamic-slice_bitcast_fusion.6), channel_id=1, source_target_pairs={{0,16},{16,0},{32,48},{48,32},{64,80},{80,64},{96,112},{112,96},{1... | collective-permute-start | bytes 491528 | tf_op jit(solution)/shard_map/ppermute | solution.py:220
  117.8 1.4 collective-permute-done.7
  119.3 0.7 slice.8
  120.1 0.6 copy.30
  120.7 25.0 %all-to-all-done.2 = bf16[16,32,1024]{2,1,0:T(8,128)(2,1)S(1)} async-done(((bf16[16,32,1024]{2,1,0:T(8,128)(2,1)}), bf16[16,32,1024]{2,1,0:T(8,128)(2,1)S(1)}, u32[]{:S(2)}, u32[]{:S(2)}) %all-to-all-start.2) | async-done | bytes 1048608 | tf_op jit(solution)/shard_map/all_to_all | solution.py:260
  145.6 1.0 copy.41
  (16 shorter events, 0.4 us)
Async XLA Ops:
  2.3 28.9 %all-to-all-start = ((bf16[16,2,32,128]{3,2,1,0:T(8,128)(2,1)}), bf16[16,2,32,128]{3,2,1,0:T(8,128)(2,1)S(1)}, u32[]{:S(2)}, u32[]{:S(2)}) async-start(bf16[16,2,32,128]{3,2,1,0:T(8,128)(2,1)} %bitcast.52), calls=%async_computation | async-start | bytes 524288 | tf_op jit(solution)/shard_map/all_to_all | solution.py:234
  19.4 11.8 %copy-start = (s32[1,32,1]{1,2,0:T(1,128)S(1)}, s32[1,32,1]{1,2,0:T(1,128)}, u32[]{:S(2)}) copy-start(s32[1,32,1]{1,2,0:T(1,128)} %param.12) | copy-start | bytes 388
  32.8 6.1 %collective-permute-start = (bf16[8,2,40,128]{3,2,1,0:T(8,128)(2,1)S(1)}, bf16[8,2,40,128]{3,2,1,0:T(8,128)(2,1)S(1)}, u32[]{:S(2)}, u32[]{:S(2)}) collective-permute-start(bf16[8,2,40,128]{3,2,1,0:T(8,128)(2,1)S(1)} %dynamic-slice_bitcast_fusion.2), channel_id=1, source_target_pairs={{16,48},{48,16},{80,112},{112,80},{144,176},{176,144},{208,240},{2... | collective-permute-start | bytes 491528 | tf_op jit(solution)/shard_map/cond/branch_1_fun/ppermute | solution.py:220
  38.9 7.6 %collective-permute-start.1 = (bf16[4,4,40,128]{3,2,1,0:T(8,128)(2,1)S(1)}, bf16[4,4,40,128]{3,2,1,0:T(8,128)(2,1)S(1)}, u32[]{:S(2)}, u32[]{:S(2)}) collective-permute-start(bf16[4,4,40,128]{3,2,1,0:T(8,128)(2,1)S(1)} %dynamic-slice_bitcast_fusion.1), channel_id=1, source_target_pairs={{16,80},{48,112},{80,16},{112,48},{144,208},{176,240},{208,144},{2... | collective-permute-start | bytes 491528 | tf_op jit(solution)/shard_map/cond/branch_1_fun/ppermute | solution.py:220
  46.6 6.1 %collective-permute-start.2 = (bf16[2,8,40,128]{3,2,1,0:T(8,128)(2,1)S(1)}, bf16[2,8,40,128]{3,2,1,0:T(8,128)(2,1)S(1)}, u32[]{:S(2)}, u32[]{:S(2)}) collective-permute-start(bf16[2,8,40,128]{3,2,1,0:T(8,128)(2,1)S(1)} %dynamic-slice_bitcast_fusion), channel_id=1, source_target_pairs={{16,144},{48,176},{80,208},{112,240},{144,16},{176,48},{208,80},{2... | collective-permute-start | bytes 491528 | tf_op jit(solution)/shard_map/cond/branch_1_fun/ppermute | solution.py:220
  57.8 40.8 %all-to-all-start.1 = ((bf16[16,32,1024]{2,1,0:T(8,128)(2,1)}), bf16[16,32,1024]{2,1,0:T(8,128)(2,1)S(1)}, u32[]{:S(2)}, u32[]{:S(2)}) async-start(bf16[16,32,1024]{2,1,0:T(8,128)(2,1)} %bitcast.158), calls=%async_computation.1 | async-start | bytes 2097152 | tf_op jit(solution)/shard_map/all_to_all | solution.py:257
  100.4 45.2 %all-to-all-start.2 = ((bf16[16,32,1024]{2,1,0:T(8,128)(2,1)}), bf16[16,32,1024]{2,1,0:T(8,128)(2,1)S(1)}, u32[]{:S(2)}, u32[]{:S(2)}) async-start(bf16[16,32,1024]{2,1,0:T(8,128)(2,1)} %hadamard.1), calls=%async_computation.2 | async-start | bytes 2097152 | tf_op jit(solution)/shard_map/all_to_all | solution.py:260
  107.9 7.9 %collective-permute-start.6 = (bf16[1,16,40,128]{3,2,1,0:T(8,128)(2,1)S(1)}, bf16[1,16,40,128]{3,2,1,0:T(8,128)(2,1)S(1)}, u32[]{:S(2)}, u32[]{:S(2)}) collective-permute-start(bf16[1,16,40,128]{3,2,1,0:T(8,128)(2,1)S(1)} %dynamic-slice_bitcast_fusion.7), channel_id=1, source_target_pairs={{0,256},{16,272},{32,288},{48,304},{64,320},{80,336},{96,352},{112... | collective-permute-start | bytes 491528 | tf_op jit(solution)/shard_map/ppermute | solution.py:220
  115.9 3.3 %collective-permute-start.7 = (bf16[16,1,40,128]{3,2,0,1:T(8,128)(2,1)S(1)}, bf16[16,1,40,128]{3,2,0,1:T(8,128)(2,1)S(1)}, u32[]{:S(2)}, u32[]{:S(2)}) collective-permute-start(bf16[16,1,40,128]{3,2,0,1:T(8,128)(2,1)S(1)} %dynamic-slice_bitcast_fusion.6), channel_id=1, source_target_pairs={{0,16},{16,0},{32,48},{48,32},{64,80},{80,64},{96,112},{112,96},{1... | collective-permute-start | bytes 491528 | tf_op jit(solution)/shard_map/ppermute | solution.py:220

commit v6 on v5

--- a/solution.py
+++ b/solution.py
@@ -160,7 +160,7 @@
     level = level_ref[0].astype(jnp.float32)
     side = side_ref[0]
     rows = lax.broadcasted_iota(jnp.int32, (PAGE, head_dim), 0)
-    tail = lax.broadcasted_iota(jnp.int32, (8, head_dim), 0)
+    tail = lax.broadcasted_iota(jnp.int32, (PAGE, head_dim), 0)
     for owner in range(owners):
         count_ref[owner] = 0
     for page in range(sources * per_source):
@@ -189,7 +189,7 @@
     smem = pl.BlockSpec(memory_space=pltpu.SMEM)
     vmem = pl.BlockSpec(memory_space=pltpu.VMEM)
     side = (lax.axis_index("tp") % 2).astype(jnp.int32).reshape(1)
-    shape = (owners, capacity * PAGE + 8, head_dim)
+    shape = (owners, (capacity + 1) * PAGE, head_dim)
     return pl.pallas_call(
         functools.partial(page_kernel, capacity=capacity),
         in_specs=[smem, smem, smem, smem, vmem],
@@ -246,7 +246,7 @@
         table = page_table(received, lengths, level, destinations[0, :, 0], owners, capacity)
         return to_owners(table, "req", first_bits, members)
 
-    shape = (owners, capacity * PAGE + 8, head_dim)
+    shape = (owners, (capacity + 1) * PAGE, head_dim)
     table = lax.cond(
         odd,
         lambda: start_pages(range(1, owners, 2)),

time: 147 us -> 147 us (level); the launches traced: 147 us -> 144 us
  waiting for transfers between devices: 78.3 us -> 72.4 us
  starting transfers between devices: 52.2 us -> 55.8 us
    all_to_all x1, waiting for transfers between devices: 25 us -> 15.4 us  [body(): back = lax.all_to_all(mixed, 'tp', split_axis=0, concat_axis=0, tiled=True)]
    all_to_all x1, starting transfers between devices: 7.5 us -> 11.3 us  [body(): back = lax.all_to_all(mixed, 'tp', split_axis=0, concat_axis=0, tiled=True)]
    all_to_all x1, waiting for transfers between devices: 28.6 us -> 30.8 us  [body(): lax.all_to_all(blocks, 'tp', split_axis=0, concat_axis=0, tiled=True)]
where the time goes in v6:
time: 147 us; the launch traced here: 144 us
  waiting for transfers between devices  72.4 us (49%)
  starting transfers between devices  55.8 us (38%)
  Pallas kernels  7.65 us (5%)
  local copies, waits for them, and re-layouts  5.11 us (3%)
  between operations  2.13 us (1%)
    all_to_all x1, waiting for transfers between devices, body(): lax.all_to_all(blocks, 'tp', split_axis=0, concat_axis=0, tiled=True)  30.8 us
    ppermute x5, starting transfers between devices, to_owners(): got = lax.ppermute(send, axis, [(i, i ^ stride) for i in members])  17.7 us
    all_to_all x1, starting transfers between devices, body(): lax.all_to_all(outgoing, 'tp', split_axis=0, concat_axis=0, tiled=True)  15.7 us
    all_to_all x1, waiting for transfers between devices, body(): back = lax.all_to_all(mixed, 'tp', split_axis=0, concat_axis=0, tiled=True)  15.4 us
    ppermute x5, waiting for transfers between devices, to_owners(): got = lax.ppermute(send, axis, [(i, i ^ stride) for i in members])  14.4 us
    all_to_all x1, waiting for transfers between devices, body(): lax.all_to_all(outgoing, 'tp', split_axis=0, concat_axis=0, tiled=True)  11.8 us
    all_to_all x1, starting transfers between devices, body(): back = lax.all_to_all(mixed, 'tp', split_axis=0, concat_axis=0, tiled=True)  11.3 us
    all_to_all x1, starting transfers between devices, body(): lax.all_to_all(blocks, 'tp', split_axis=0, concat_axis=0, tiled=True)  11 us
  transfers between devices with their start and end apart: 8, of which 8 were waited for; matrix products, arithmetic and copies ran while one was open for 2% of the time, Pallas kernels for 0%

profile of v6, /device:TPU:1, one launch (start us, length us, event | category | flops | bytes accessed | tf_op | source)
XLA Modules:
  0.0 144.3 jit_solution(4695420772604406621)
XLA Ops:
  0.6 1.7 %broadcast_in_dim.7 = bf16[8,2,2,32,128]{4,3,2,1,0:T(8,128)(2,1)} broadcast(bf16[8,2,32,128]{3,2,1,0:T(8,128)(2,1)} %bitcast.160), dimensions={0,2,3,4} | broadcast | bytes 393216 | tf_op jit(solution)/shard_map/broadcast_in_dim | solution.py:233
  2.3 15.7 %all-to-all-start = ((bf16[16,2,32,128]{3,2,1,0:T(8,128)(2,1)}), bf16[16,2,32,128]{3,2,1,0:T(8,128)(2,1)S(1)}, u32[]{:S(2)}, u32[]{:S(2)}) async-start(bf16[16,2,32,128]{3,2,1,0:T(8,128)(2,1)} %bitcast.52), calls=%async_computation | async-start | bytes 524288 | tf_op jit(solution)/shard_map/all_to_all | solution.py:234
  19.4 0.0 copy-start
  19.4 11.8 %all-to-all-done.kv_ref = bf16[16,2,32,128]{3,2,1,0:T(8,128)(2,1)S(1)} async-done(((bf16[16,2,32,128]{3,2,1,0:T(8,128)(2,1)}), bf16[16,2,32,128]{3,2,1,0:T(8,128)(2,1)S(1)}, u32[]{:S(2)}, u32[]{:S(2)}) %all-to-all-start) | async-done | bytes 262176 | tf_op jit(solution)/shard_map/all_to_all | solution.py:234
  31.2 0.0 copy-done
  31.2 23.7 %conditional.2 = (bf16[32,48,128]{2,1,0:T(8,128)(2,1)}) conditional(s32[]{:T(128)} %convert_element_type.4, () %tuple.24, (s32[1,32,1]{1,2,0:T(1,128)S(1)}, s32[1]{0:T(128)}, s32[1]{0:T(128)}, bf16[16,2,32,128]{3,2,1,0:T(8,128)(2,1)S(1)}) %tuple.43), branch_computations={%region_0.1_spmd, %region_1.2_spmd} | conditional | flops 2490444 | bytes 8520626 | solution.py:250
  31.2 1.6 %pages.2 = bf16[32,48,128]{2,1,0:T(8,128)(2,1)S(1)} custom-call(s32[1]{0:T(128)} %get-tuple-element.23.length_ref, s32[1]{0:T(128)} %get-tuple-element.24.level_ref, s32[1]{0:T(128)} %bitcast.side_ref, s32[32]{0:T(128)S(1)} %bitcast.161, bf16[16,2,32,128]{3,2,1,0:T(8,128)(2,1)S(1)} %get-tuple-element.26.kv_ref), custom_call_target="tpu_custom_call" | custom-call | flops 1310720 | bytes 262144 | tf_op jit(solution)/shard_map/cond/branch_1_fun/pages/pallas_call | solution.py:193
  32.8 3.1 %collective-permute-start = (bf16[8,2,48,128]{3,2,1,0:T(8,128)(2,1)S(1)}, bf16[8,2,48,128]{3,2,1,0:T(8,128)(2,1)S(1)}, u32[]{:S(2)}, u32[]{:S(2)}) collective-permute-start(bf16[8,2,48,128]{3,2,1,0:T(8,128)(2,1)S(1)} %dynamic-slice_bitcast_fusion.2), channel_id=1, source_target_pairs={{16,48},{48,16},{80,112},{112,80},{144,176},{176,144},{208,240},{2... | collective-permute-start | bytes 589832 | tf_op jit(solution)/shard_map/cond/branch_1_fun/ppermute | solution.py:220
  35.9 3.3 %collective-permute-done = bf16[8,2,48,128]{3,2,1,0:T(8,128)(2,1)S(1)} collective-permute-done((bf16[8,2,48,128]{3,2,1,0:T(8,128)(2,1)S(1)}, bf16[8,2,48,128]{3,2,1,0:T(8,128)(2,1)S(1)}, u32[]{:S(2)}, u32[]{:S(2)}) %collective-permute-start) | collective-permute-done | bytes 196640 | tf_op jit(solution)/shard_map/cond/branch_1_fun/ppermute | solution.py:220
  39.3 4.7 %collective-permute-start.1 = (bf16[4,4,48,128]{3,2,1,0:T(8,128)(2,1)S(1)}, bf16[4,4,48,128]{3,2,1,0:T(8,128)(2,1)S(1)}, u32[]{:S(2)}, u32[]{:S(2)}) collective-permute-start(bf16[4,4,48,128]{3,2,1,0:T(8,128)(2,1)S(1)} %dynamic-slice_bitcast_fusion.1), channel_id=1, source_target_pairs={{16,80},{48,112},{80,16},{112,48},{144,208},{176,240},{208,144},{2... | collective-permute-start | bytes 589832 | tf_op jit(solution)/shard_map/cond/branch_1_fun/ppermute | solution.py:220
  44.0 3.2 %collective-permute-done.1 = bf16[4,4,48,128]{3,2,1,0:T(8,128)(2,1)S(1)} collective-permute-done((bf16[4,4,48,128]{3,2,1,0:T(8,128)(2,1)S(1)}, bf16[4,4,48,128]{3,2,1,0:T(8,128)(2,1)S(1)}, u32[]{:S(2)}, u32[]{:S(2)}) %collective-permute-start.1) | collective-permute-done | bytes 196640 | tf_op jit(solution)/shard_map/cond/branch_1_fun/ppermute | solution.py:220
  47.3 3.2 %collective-permute-start.2 = (bf16[2,8,48,128]{3,2,1,0:T(8,128)(2,1)S(1)}, bf16[2,8,48,128]{3,2,1,0:T(8,128)(2,1)S(1)}, u32[]{:S(2)}, u32[]{:S(2)}) collective-permute-start(bf16[2,8,48,128]{3,2,1,0:T(8,128)(2,1)S(1)} %dynamic-slice_bitcast_fusion), channel_id=1, source_target_pairs={{16,144},{48,176},{80,208},{112,240},{144,16},{176,48},{208,80},{2... | collective-permute-start | bytes 589832 | tf_op jit(solution)/shard_map/cond/branch_1_fun/ppermute | solution.py:220
  50.5 3.5 %collective-permute-done.2 = bf16[2,8,48,128]{3,2,1,0:T(8,128)(2,1)S(1)} collective-permute-done((bf16[2,8,48,128]{3,2,1,0:T(8,128)(2,1)S(1)}, bf16[2,8,48,128]{3,2,1,0:T(8,128)(2,1)S(1)}, u32[]{:S(2)}, u32[]{:S(2)}) %collective-permute-start.2) | collective-permute-done | bytes 196640 | tf_op jit(solution)/shard_map/cond/branch_1_fun/ppermute | solution.py:220
  54.1 0.8 pad_maximum_fusion.2
  54.9 4.3 %attend.1 = bf16[512,1024]{1,0:T(8,128)(2,1)} custom-call(s32[1]{0:T(128)S(6)} %copy.40.length_ref, bf16[512,1024]{1,0:T(8,128)(2,1)} %bitcast.164, bf16[16,2,32,128]{3,2,1,0:T(8,128)(2,1)S(1)} %all-to-all-done.kv_ref, bf16[32,48,128]{2,1,0:T(8,128)(2,1)} %get-tuple-element.70.after_ref), custom_call_target="tpu_custom_call" | custom-call | flops 1073741824 | bytes 2097152 | tf_op jit(solution)/shard_map/attend/pallas_call | solution.py:71
  59.2 11.0 %all-to-all-start.1 = ((bf16[16,32,1024]{2,1,0:T(8,128)(2,1)}), bf16[16,32,1024]{2,1,0:T(8,128)(2,1)S(1)}, u32[]{:S(2)}, u32[]{:S(2)}) async-start(bf16[16,32,1024]{2,1,0:T(8,128)(2,1)} %bitcast.158), calls=%async_computation.1 | async-start | bytes 2097152 | tf_op jit(solution)/shard_map/all_to_all | solution.py:257
  70.1 1.0 conditional.3
  70.2 1.0 copy.37
  71.2 30.8 %all-to-all-done.1.in_ref = bf16[16,32,1024]{2,1,0:T(8,128)(2,1)S(1)} async-done(((bf16[16,32,1024]{2,1,0:T(8,128)(2,1)}), bf16[16,32,1024]{2,1,0:T(8,128)(2,1)S(1)}, u32[]{:S(2)}, u32[]{:S(2)}) %all-to-all-start.1) | async-done | bytes 1048608 | tf_op jit(solution)/shard_map/all_to_all | solution.py:257
  101.9 1.8 %hadamard.1 = bf16[16,32,1024]{2,1,0:T(8,128)(2,1)} custom-call(bf16[16,32,1024]{2,1,0:T(8,128)(2,1)S(1)} %all-to-all-done.1.in_ref, bf16[32,48,128]{2,1,0:T(8,128)(2,1)} %get-tuple-element.36.after_ref), custom_call_target="tpu_custom_call" | custom-call | flops 3670016 | bytes 2097152 | tf_op jit(solution)/shard_map/hadamard/pallas_call | solution.py:138
  103.7 11.3 %all-to-all-start.2 = ((bf16[16,32,1024]{2,1,0:T(8,128)(2,1)}), bf16[16,32,1024]{2,1,0:T(8,128)(2,1)S(1)}, u32[]{:S(2)}, u32[]{:S(2)}) async-start(bf16[16,32,1024]{2,1,0:T(8,128)(2,1)} %hadamard.1), calls=%async_computation.2 | async-start | bytes 2097152 | tf_op jit(solution)/shard_map/all_to_all | solution.py:260
  115.1 4.8 %collective-permute-start.6 = (bf16[1,16,48,128]{3,2,1,0:T(8,128)(2,1)S(1)}, bf16[1,16,48,128]{3,2,1,0:T(8,128)(2,1)S(1)}, u32[]{:S(2)}, u32[]{:S(2)}) collective-permute-start(bf16[1,16,48,128]{3,2,1,0:T(8,128)(2,1)S(1)} %dynamic-slice_bitcast_fusion.7), channel_id=1, source_target_pairs={{0,256},{16,272},{32,288},{48,304},{64,320},{80,336},{96,352},{112... | collective-permute-start | bytes 589832 | tf_op jit(solution)/shard_map/ppermute | solution.py:220
  120.0 3.0 %collective-permute-done.6 = bf16[1,16,48,128]{3,2,1,0:T(8,128)(2,1)S(1)} collective-permute-done((bf16[1,16,48,128]{3,2,1,0:T(8,128)(2,1)S(1)}, bf16[1,16,48,128]{3,2,1,0:T(8,128)(2,1)S(1)}, u32[]{:S(2)}, u32[]{:S(2)}) %collective-permute-start.6) | collective-permute-done | bytes 196640 | tf_op jit(solution)/shard_map/ppermute | solution.py:220
  123.1 1.9 %collective-permute-start.7 = (bf16[16,1,48,128]{3,2,0,1:T(8,128)(2,1)S(1)}, bf16[16,1,48,128]{3,2,0,1:T(8,128)(2,1)S(1)}, u32[]{:S(2)}, u32[]{:S(2)}) collective-permute-start(bf16[16,1,48,128]{3,2,0,1:T(8,128)(2,1)S(1)} %dynamic-slice_bitcast_fusion.6), channel_id=1, source_target_pairs={{0,16},{16,0},{32,48},{48,32},{64,80},{80,64},{96,112},{112,96},{1... | collective-permute-start | bytes 589832 | tf_op jit(solution)/shard_map/ppermute | solution.py:220
  125.1 1.4 collective-permute-done.7
  126.6 0.7 slice.8
  127.3 0.6 copy.30
  127.9 15.4 %all-to-all-done.2 = bf16[16,32,1024]{2,1,0:T(8,128)(2,1)S(1)} async-done(((bf16[16,32,1024]{2,1,0:T(8,128)(2,1)}), bf16[16,32,1024]{2,1,0:T(8,128)(2,1)S(1)}, u32[]{:S(2)}, u32[]{:S(2)}) %all-to-all-start.2) | async-done | bytes 1048608 | tf_op jit(solution)/shard_map/all_to_all | solution.py:260
  143.3 1.0 copy.41
  (16 shorter events, 0.5 us)
Async XLA Ops:
  2.3 28.9 %all-to-all-start = ((bf16[16,2,32,128]{3,2,1,0:T(8,128)(2,1)}), bf16[16,2,32,128]{3,2,1,0:T(8,128)(2,1)S(1)}, u32[]{:S(2)}, u32[]{:S(2)}) async-start(bf16[16,2,32,128]{3,2,1,0:T(8,128)(2,1)} %bitcast.52), calls=%async_computation | async-start | bytes 524288 | tf_op jit(solution)/shard_map/all_to_all | solution.py:234
  19.4 11.8 %copy-start = (s32[1,32,1]{1,2,0:T(1,128)S(1)}, s32[1,32,1]{1,2,0:T(1,128)}, u32[]{:S(2)}) copy-start(s32[1,32,1]{1,2,0:T(1,128)} %param.12) | copy-start | bytes 388
  32.8 6.4 %collective-permute-start = (bf16[8,2,48,128]{3,2,1,0:T(8,128)(2,1)S(1)}, bf16[8,2,48,128]{3,2,1,0:T(8,128)(2,1)S(1)}, u32[]{:S(2)}, u32[]{:S(2)}) collective-permute-start(bf16[8,2,48,128]{3,2,1,0:T(8,128)(2,1)S(1)} %dynamic-slice_bitcast_fusion.2), channel_id=1, source_target_pairs={{16,48},{48,16},{80,112},{112,80},{144,176},{176,144},{208,240},{2... | collective-permute-start | bytes 589832 | tf_op jit(solution)/shard_map/cond/branch_1_fun/ppermute | solution.py:220
  39.3 7.9 %collective-permute-start.1 = (bf16[4,4,48,128]{3,2,1,0:T(8,128)(2,1)S(1)}, bf16[4,4,48,128]{3,2,1,0:T(8,128)(2,1)S(1)}, u32[]{:S(2)}, u32[]{:S(2)}) collective-permute-start(bf16[4,4,48,128]{3,2,1,0:T(8,128)(2,1)S(1)} %dynamic-slice_bitcast_fusion.1), channel_id=1, source_target_pairs={{16,80},{48,112},{80,16},{112,48},{144,208},{176,240},{208,144},{2... | collective-permute-start | bytes 589832 | tf_op jit(solution)/shard_map/cond/branch_1_fun/ppermute | solution.py:220
  47.3 6.7 %collective-permute-start.2 = (bf16[2,8,48,128]{3,2,1,0:T(8,128)(2,1)S(1)}, bf16[2,8,48,128]{3,2,1,0:T(8,128)(2,1)S(1)}, u32[]{:S(2)}, u32[]{:S(2)}) collective-permute-start(bf16[2,8,48,128]{3,2,1,0:T(8,128)(2,1)S(1)} %dynamic-slice_bitcast_fusion), channel_id=1, source_target_pairs={{16,144},{48,176},{80,208},{112,240},{144,16},{176,48},{208,80},{2... | collective-permute-start | bytes 589832 | tf_op jit(solution)/shard_map/cond/branch_1_fun/ppermute | solution.py:220
  59.2 42.8 %all-to-all-start.1 = ((bf16[16,32,1024]{2,1,0:T(8,128)(2,1)}), bf16[16,32,1024]{2,1,0:T(8,128)(2,1)S(1)}, u32[]{:S(2)}, u32[]{:S(2)}) async-start(bf16[16,32,1024]{2,1,0:T(8,128)(2,1)} %bitcast.158), calls=%async_computation.1 | async-start | bytes 2097152 | tf_op jit(solution)/shard_map/all_to_all | solution.py:257
  103.7 39.6 %all-to-all-start.2 = ((bf16[16,32,1024]{2,1,0:T(8,128)(2,1)}), bf16[16,32,1024]{2,1,0:T(8,128)(2,1)S(1)}, u32[]{:S(2)}, u32[]{:S(2)}) async-start(bf16[16,32,1024]{2,1,0:T(8,128)(2,1)} %hadamard.1), calls=%async_computation.2 | async-start | bytes 2097152 | tf_op jit(solution)/shard_map/all_to_all | solution.py:260
  115.1 7.9 %collective-permute-start.6 = (bf16[1,16,48,128]{3,2,1,0:T(8,128)(2,1)S(1)}, bf16[1,16,48,128]{3,2,1,0:T(8,128)(2,1)S(1)}, u32[]{:S(2)}, u32[]{:S(2)}) collective-permute-start(bf16[1,16,48,128]{3,2,1,0:T(8,128)(2,1)S(1)} %dynamic-slice_bitcast_fusion.7), channel_id=1, source_target_pairs={{0,256},{16,272},{32,288},{48,304},{64,320},{80,336},{96,352},{112... | collective-permute-start | bytes 589832 | tf_op jit(solution)/shard_map/ppermute | solution.py:220
  123.1 3.3 %collective-permute-start.7 = (bf16[16,1,48,128]{3,2,0,1:T(8,128)(2,1)S(1)}, bf16[16,1,48,128]{3,2,0,1:T(8,128)(2,1)S(1)}, u32[]{:S(2)}, u32[]{:S(2)}) collective-permute-start(bf16[16,1,48,128]{3,2,0,1:T(8,128)(2,1)S(1)} %dynamic-slice_bitcast_fusion.6), channel_id=1, source_target_pairs={{0,16},{16,0},{32,48},{48,32},{64,80},{80,64},{96,112},{112,96},{1... | collective-permute-start | bytes 589832 | tf_op jit(solution)/shard_map/ppermute | solution.py:220

commit v7 on v6

--- a/solution.py
+++ b/solution.py
@@ -133,13 +133,11 @@
 
 
 def hadamard(blocks, heads, after):
-    devices, tokens, width = blocks.shape
-    spec = pl.BlockSpec((devices, PAGE, width), lambda i: (0, i, 0))
+    devices, _, width = blocks.shape
     return pl.pallas_call(
         functools.partial(hadamard_kernel, heads=heads),
-        grid=(tokens // PAGE,),
-        in_specs=[spec, pl.BlockSpec(memory_space=pl.ANY)],
-        out_specs=spec,
+        in_specs=[VMEM, ANYWHERE],
+        out_specs=VMEM,
         out_shape=jax.ShapeDtypeStruct(blocks.shape, jnp.bfloat16),
         scratch_shapes=[pltpu.VMEM((devices, PAGE, width), jnp.float32)],
         compiler_params=pltpu.CompilerParams(vmem_limit_bytes=32 * 1024 * 1024),

time: 147 us -> 147 us (level)
  the two profiles are of different devices: /device:TPU:1 before, /device:TPU:57 now
where the time goes in v7:
time: 147 us; the launch traced here: 146 us
  waiting for transfers between devices  78.3 us (53%)
  starting transfers between devices  52 us (35%)
  Pallas kernels  7.74 us (5%)
  local copies, waits for them, and re-layouts  5.1 us (3%)
  between operations  2.08 us (1%)
    all_to_all x1, waiting for transfers between devices, body(): lax.all_to_all(blocks, 'tp', split_axis=0, concat_axis=0, tiled=True)  26.1 us
    all_to_all x1, waiting for transfers between devices, body(): back = lax.all_to_all(mixed, 'tp', split_axis=0, concat_axis=0, tiled=True)  18.7 us
    ppermute x5, waiting for transfers between devices, to_owners(): got = lax.ppermute(send, axis, [(i, i ^ stride) for i in members])  17.2 us
    all_to_all x1, waiting for transfers between devices, body(): lax.all_to_all(outgoing, 'tp', split_axis=0, concat_axis=0, tiled=True)  16.3 us
    all_to_all x1, starting transfers between devices, body(): back = lax.all_to_all(mixed, 'tp', split_axis=0, concat_axis=0, tiled=True)  16 us
    ppermute x5, starting transfers between devices, to_owners(): got = lax.ppermute(send, axis, [(i, i ^ stride) for i in members])  14.9 us
    all_to_all x1, starting transfers between devices, body(): lax.all_to_all(outgoing, 'tp', split_axis=0, concat_axis=0, tiled=True)  14.7 us
    all_to_all x1, starting transfers between devices, body(): lax.all_to_all(blocks, 'tp', split_axis=0, concat_axis=0, tiled=True)  6.48 us
  transfers between devices with their start and end apart: 8, of which 8 were waited for; matrix products, arithmetic and copies ran while one was open for 2% of the time, Pallas kernels for 0%

profile of v7, /device:TPU:57, one launch (start us, length us, event | category | flops | bytes accessed | tf_op | source)
XLA Modules:
  0.0 146.5 jit_solution(4649838382790331316)
XLA Ops:
  0.6 1.7 %broadcast_in_dim.7 = bf16[8,2,2,32,128]{4,3,2,1,0:T(8,128)(2,1)} broadcast(bf16[8,2,32,128]{3,2,1,0:T(8,128)(2,1)} %bitcast.160), dimensions={0,2,3,4} | broadcast | bytes 393216 | tf_op jit(solution)/shard_map/broadcast_in_dim | solution.py:231
  2.3 14.7 %all-to-all-start = ((bf16[16,2,32,128]{3,2,1,0:T(8,128)(2,1)}), bf16[16,2,32,128]{3,2,1,0:T(8,128)(2,1)S(1)}, u32[]{:S(2)}, u32[]{:S(2)}) async-start(bf16[16,2,32,128]{3,2,1,0:T(8,128)(2,1)} %bitcast.52), calls=%async_computation | async-start | bytes 524288 | tf_op jit(solution)/shard_map/all_to_all | solution.py:232
  18.3 0.0 copy-start
  18.3 16.3 %all-to-all-done.kv_ref = bf16[16,2,32,128]{3,2,1,0:T(8,128)(2,1)S(1)} async-done(((bf16[16,2,32,128]{3,2,1,0:T(8,128)(2,1)}), bf16[16,2,32,128]{3,2,1,0:T(8,128)(2,1)S(1)}, u32[]{:S(2)}, u32[]{:S(2)}) %all-to-all-start) | async-done | bytes 262176 | tf_op jit(solution)/shard_map/all_to_all | solution.py:232
  34.6 0.0 copy-done
  34.6 23.7 %conditional.2 = (bf16[32,48,128]{2,1,0:T(8,128)(2,1)}) conditional(s32[]{:T(128)} %convert_element_type.4, () %tuple.24, (s32[1,32,1]{1,2,0:T(1,128)S(1)}, s32[1]{0:T(128)}, s32[1]{0:T(128)}, bf16[16,2,32,128]{3,2,1,0:T(8,128)(2,1)S(1)}) %tuple.43), branch_computations={%region_0.1_spmd, %region_1.2_spmd} | conditional | flops 2490444 | bytes 8520626 | solution.py:248
  34.6 1.6 %pages.2 = bf16[32,48,128]{2,1,0:T(8,128)(2,1)S(1)} custom-call(s32[1]{0:T(128)} %get-tuple-element.23.length_ref, s32[1]{0:T(128)} %get-tuple-element.24.level_ref, s32[1]{0:T(128)} %bitcast.side_ref, s32[32]{0:T(128)S(1)} %bitcast.161, bf16[16,2,32,128]{3,2,1,0:T(8,128)(2,1)S(1)} %get-tuple-element.26.kv_ref), custom_call_target="tpu_custom_call" | custom-call | flops 1310720 | bytes 262144 | tf_op jit(solution)/shard_map/cond/branch_1_fun/pages/pallas_call | solution.py:191
  36.2 3.1 %collective-permute-start = (bf16[8,2,48,128]{3,2,1,0:T(8,128)(2,1)S(1)}, bf16[8,2,48,128]{3,2,1,0:T(8,128)(2,1)S(1)}, u32[]{:S(2)}, u32[]{:S(2)}) collective-permute-start(bf16[8,2,48,128]{3,2,1,0:T(8,128)(2,1)S(1)} %dynamic-slice_bitcast_fusion.2), channel_id=1, source_target_pairs={{16,48},{48,16},{80,112},{112,80},{144,176},{176,144},{208,240},{2... | collective-permute-start | bytes 589832 | tf_op jit(solution)/shard_map/cond/branch_1_fun/ppermute | solution.py:218
  39.3 3.3 %collective-permute-done = bf16[8,2,48,128]{3,2,1,0:T(8,128)(2,1)S(1)} collective-permute-done((bf16[8,2,48,128]{3,2,1,0:T(8,128)(2,1)S(1)}, bf16[8,2,48,128]{3,2,1,0:T(8,128)(2,1)S(1)}, u32[]{:S(2)}, u32[]{:S(2)}) %collective-permute-start) | collective-permute-done | bytes 196640 | tf_op jit(solution)/shard_map/cond/branch_1_fun/ppermute | solution.py:218
  42.7 4.7 %collective-permute-start.1 = (bf16[4,4,48,128]{3,2,1,0:T(8,128)(2,1)S(1)}, bf16[4,4,48,128]{3,2,1,0:T(8,128)(2,1)S(1)}, u32[]{:S(2)}, u32[]{:S(2)}) collective-permute-start(bf16[4,4,48,128]{3,2,1,0:T(8,128)(2,1)S(1)} %dynamic-slice_bitcast_fusion.1), channel_id=1, source_target_pairs={{16,80},{48,112},{80,16},{112,48},{144,208},{176,240},{208,144},{2... | collective-permute-start | bytes 589832 | tf_op jit(solution)/shard_map/cond/branch_1_fun/ppermute | solution.py:218
  47.4 3.2 %collective-permute-done.1 = bf16[4,4,48,128]{3,2,1,0:T(8,128)(2,1)S(1)} collective-permute-done((bf16[4,4,48,128]{3,2,1,0:T(8,128)(2,1)S(1)}, bf16[4,4,48,128]{3,2,1,0:T(8,128)(2,1)S(1)}, u32[]{:S(2)}, u32[]{:S(2)}) %collective-permute-start.1) | collective-permute-done | bytes 196640 | tf_op jit(solution)/shard_map/cond/branch_1_fun/ppermute | solution.py:218
  50.7 2.4 %collective-permute-start.2 = (bf16[2,8,48,128]{3,2,1,0:T(8,128)(2,1)S(1)}, bf16[2,8,48,128]{3,2,1,0:T(8,128)(2,1)S(1)}, u32[]{:S(2)}, u32[]{:S(2)}) collective-permute-start(bf16[2,8,48,128]{3,2,1,0:T(8,128)(2,1)S(1)} %dynamic-slice_bitcast_fusion), channel_id=1, source_target_pairs={{16,144},{48,176},{80,208},{112,240},{144,16},{176,48},{208,80},{2... | collective-permute-start | bytes 589832 | tf_op jit(solution)/shard_map/cond/branch_1_fun/ppermute | solution.py:218
  53.1 4.3 %collective-permute-done.2 = bf16[2,8,48,128]{3,2,1,0:T(8,128)(2,1)S(1)} collective-permute-done((bf16[2,8,48,128]{3,2,1,0:T(8,128)(2,1)S(1)}, bf16[2,8,48,128]{3,2,1,0:T(8,128)(2,1)S(1)}, u32[]{:S(2)}, u32[]{:S(2)}) %collective-permute-start.2) | collective-permute-done | bytes 196640 | tf_op jit(solution)/shard_map/cond/branch_1_fun/ppermute | solution.py:218
  57.5 0.8 pad_maximum_fusion.2
  58.2 4.3 %attend.1 = bf16[512,1024]{1,0:T(8,128)(2,1)} custom-call(s32[1]{0:T(128)S(6)} %copy.40.length_ref, bf16[512,1024]{1,0:T(8,128)(2,1)} %bitcast.164, bf16[16,2,32,128]{3,2,1,0:T(8,128)(2,1)S(1)} %all-to-all-done.kv_ref, bf16[32,48,128]{2,1,0:T(8,128)(2,1)} %get-tuple-element.70.after_ref), custom_call_target="tpu_custom_call" | custom-call | flops 1073741824 | bytes 2097152 | tf_op jit(solution)/shard_map/attend/pallas_call | solution.py:71
  62.6 6.5 %all-to-all-start.1 = ((bf16[16,32,1024]{2,1,0:T(8,128)(2,1)}), bf16[16,32,1024]{2,1,0:T(8,128)(2,1)S(1)}, u32[]{:S(2)}, u32[]{:S(2)}) async-start(bf16[16,32,1024]{2,1,0:T(8,128)(2,1)} %bitcast.158), calls=%async_computation.1 | async-start | bytes 2097152 | tf_op jit(solution)/shard_map/all_to_all | solution.py:255
  69.0 1.0 conditional.3
  69.0 1.0 copy.37
  70.0 26.1 %all-to-all-done.1.in_ref = bf16[16,32,1024]{2,1,0:T(8,128)(2,1)S(1)} async-done(((bf16[16,32,1024]{2,1,0:T(8,128)(2,1)}), bf16[16,32,1024]{2,1,0:T(8,128)(2,1)S(1)}, u32[]{:S(2)}, u32[]{:S(2)}) %all-to-all-start.1) | async-done | bytes 1048608 | tf_op jit(solution)/shard_map/all_to_all | solution.py:255
  96.1 1.9 %hadamard.1 = bf16[16,32,1024]{2,1,0:T(8,128)(2,1)} custom-call(bf16[16,32,1024]{2,1,0:T(8,128)(2,1)S(1)} %all-to-all-done.1.in_ref, bf16[32,48,128]{2,1,0:T(8,128)(2,1)} %get-tuple-element.36.after_ref), custom_call_target="tpu_custom_call" | custom-call | flops 3670016 | bytes 2097152 | tf_op jit(solution)/shard_map/hadamard/pallas_call | solution.py:137
  98.0 16.0 %all-to-all-start.2 = ((bf16[16,32,1024]{2,1,0:T(8,128)(2,1)}), bf16[16,32,1024]{2,1,0:T(8,128)(2,1)S(1)}, u32[]{:S(2)}, u32[]{:S(2)}) async-start(bf16[16,32,1024]{2,1,0:T(8,128)(2,1)} %hadamard.1), calls=%async_computation.2 | async-start | bytes 2097152 | tf_op jit(solution)/shard_map/all_to_all | solution.py:258
  114.0 2.9 %collective-permute-start.6 = (bf16[1,16,48,128]{3,2,1,0:T(8,128)(2,1)S(1)}, bf16[1,16,48,128]{3,2,1,0:T(8,128)(2,1)S(1)}, u32[]{:S(2)}, u32[]{:S(2)}) collective-permute-start(bf16[1,16,48,128]{3,2,1,0:T(8,128)(2,1)S(1)} %dynamic-slice_bitcast_fusion.7), channel_id=1, source_target_pairs={{0,256},{16,272},{32,288},{48,304},{64,320},{80,336},{96,352},{112... | collective-permute-start | bytes 589832 | tf_op jit(solution)/shard_map/ppermute | solution.py:218
  116.9 5.0 %collective-permute-done.6 = bf16[1,16,48,128]{3,2,1,0:T(8,128)(2,1)S(1)} collective-permute-done((bf16[1,16,48,128]{3,2,1,0:T(8,128)(2,1)S(1)}, bf16[1,16,48,128]{3,2,1,0:T(8,128)(2,1)S(1)}, u32[]{:S(2)}, u32[]{:S(2)}) %collective-permute-start.6) | collective-permute-done | bytes 196640 | tf_op jit(solution)/shard_map/ppermute | solution.py:218
  122.0 1.9 %collective-permute-start.7 = (bf16[16,1,48,128]{3,2,0,1:T(8,128)(2,1)S(1)}, bf16[16,1,48,128]{3,2,0,1:T(8,128)(2,1)S(1)}, u32[]{:S(2)}, u32[]{:S(2)}) collective-permute-start(bf16[16,1,48,128]{3,2,0,1:T(8,128)(2,1)S(1)} %dynamic-slice_bitcast_fusion.6), channel_id=1, source_target_pairs={{0,16},{16,0},{32,48},{48,32},{64,80},{80,64},{96,112},{112,96},{1... | collective-permute-start | bytes 589832 | tf_op jit(solution)/shard_map/ppermute | solution.py:218
  123.9 1.4 collective-permute-done.7
  125.5 0.7 slice.8
  126.2 0.6 copy.30
  126.8 18.7 %all-to-all-done.2 = bf16[16,32,1024]{2,1,0:T(8,128)(2,1)S(1)} async-done(((bf16[16,32,1024]{2,1,0:T(8,128)(2,1)}), bf16[16,32,1024]{2,1,0:T(8,128)(2,1)S(1)}, u32[]{:S(2)}, u32[]{:S(2)}) %all-to-all-start.2) | async-done | bytes 1048608 | tf_op jit(solution)/shard_map/all_to_all | solution.py:258
  145.5 1.0 copy.41
  (16 shorter events, 0.5 us)
Async XLA Ops:
  2.3 32.3 %all-to-all-start = ((bf16[16,2,32,128]{3,2,1,0:T(8,128)(2,1)}), bf16[16,2,32,128]{3,2,1,0:T(8,128)(2,1)S(1)}, u32[]{:S(2)}, u32[]{:S(2)}) async-start(bf16[16,2,32,128]{3,2,1,0:T(8,128)(2,1)} %bitcast.52), calls=%async_computation | async-start | bytes 524288 | tf_op jit(solution)/shard_map/all_to_all | solution.py:232
  18.3 16.3 %copy-start = (s32[1,32,1]{1,2,0:T(1,128)S(1)}, s32[1,32,1]{1,2,0:T(1,128)}, u32[]{:S(2)}) copy-start(s32[1,32,1]{1,2,0:T(1,128)} %param.12) | copy-start | bytes 388
  36.2 6.4 %collective-permute-start = (bf16[8,2,48,128]{3,2,1,0:T(8,128)(2,1)S(1)}, bf16[8,2,48,128]{3,2,1,0:T(8,128)(2,1)S(1)}, u32[]{:S(2)}, u32[]{:S(2)}) collective-permute-start(bf16[8,2,48,128]{3,2,1,0:T(8,128)(2,1)S(1)} %dynamic-slice_bitcast_fusion.2), channel_id=1, source_target_pairs={{16,48},{48,16},{80,112},{112,80},{144,176},{176,144},{208,240},{2... | collective-permute-start | bytes 589832 | tf_op jit(solution)/shard_map/cond/branch_1_fun/ppermute | solution.py:218
  42.7 7.9 %collective-permute-start.1 = (bf16[4,4,48,128]{3,2,1,0:T(8,128)(2,1)S(1)}, bf16[4,4,48,128]{3,2,1,0:T(8,128)(2,1)S(1)}, u32[]{:S(2)}, u32[]{:S(2)}) collective-permute-start(bf16[4,4,48,128]{3,2,1,0:T(8,128)(2,1)S(1)} %dynamic-slice_bitcast_fusion.1), channel_id=1, source_target_pairs={{16,80},{48,112},{80,16},{112,48},{144,208},{176,240},{208,144},{2... | collective-permute-start | bytes 589832 | tf_op jit(solution)/shard_map/cond/branch_1_fun/ppermute | solution.py:218
  50.7 6.7 %collective-permute-start.2 = (bf16[2,8,48,128]{3,2,1,0:T(8,128)(2,1)S(1)}, bf16[2,8,48,128]{3,2,1,0:T(8,128)(2,1)S(1)}, u32[]{:S(2)}, u32[]{:S(2)}) collective-permute-start(bf16[2,8,48,128]{3,2,1,0:T(8,128)(2,1)S(1)} %dynamic-slice_bitcast_fusion), channel_id=1, source_target_pairs={{16,144},{48,176},{80,208},{112,240},{144,16},{176,48},{208,80},{2... | collective-permute-start | bytes 589832 | tf_op jit(solution)/shard_map/cond/branch_1_fun/ppermute | solution.py:218
  62.6 33.6 %all-to-all-start.1 = ((bf16[16,32,1024]{2,1,0:T(8,128)(2,1)}), bf16[16,32,1024]{2,1,0:T(8,128)(2,1)S(1)}, u32[]{:S(2)}, u32[]{:S(2)}) async-start(bf16[16,32,1024]{2,1,0:T(8,128)(2,1)} %bitcast.158), calls=%async_computation.1 | async-start | bytes 2097152 | tf_op jit(solution)/shard_map/all_to_all | solution.py:255
  98.0 47.5 %all-to-all-start.2 = ((bf16[16,32,1024]{2,1,0:T(8,128)(2,1)}), bf16[16,32,1024]{2,1,0:T(8,128)(2,1)S(1)}, u32[]{:S(2)}, u32[]{:S(2)}) async-start(bf16[16,32,1024]{2,1,0:T(8,128)(2,1)} %hadamard.1), calls=%async_computation.2 | async-start | bytes 2097152 | tf_op jit(solution)/shard_map/all_to_all | solution.py:258
  114.0 7.9 %collective-permute-start.6 = (bf16[1,16,48,128]{3,2,1,0:T(8,128)(2,1)S(1)}, bf16[1,16,48,128]{3,2,1,0:T(8,128)(2,1)S(1)}, u32[]{:S(2)}, u32[]{:S(2)}) collective-permute-start(bf16[1,16,48,128]{3,2,1,0:T(8,128)(2,1)S(1)} %dynamic-slice_bitcast_fusion.7), channel_id=1, source_target_pairs={{0,256},{16,272},{32,288},{48,304},{64,320},{80,336},{96,352},{112... | collective-permute-start | bytes 589832 | tf_op jit(solution)/shard_map/ppermute | solution.py:218
  122.0 3.3 %collective-permute-start.7 = (bf16[16,1,48,128]{3,2,0,1:T(8,128)(2,1)S(1)}, bf16[16,1,48,128]{3,2,0,1:T(8,128)(2,1)S(1)}, u32[]{:S(2)}, u32[]{:S(2)}) collective-permute-start(bf16[16,1,48,128]{3,2,0,1:T(8,128)(2,1)S(1)} %dynamic-slice_bitcast_fusion.6), channel_id=1, source_target_pairs={{0,16},{16,0},{32,48},{48,32},{64,80},{80,64},{96,112},{112,96},{1... | collective-permute-start | bytes 589832 | tf_op jit(solution)/shard_map/ppermute | solution.py:218
